TPU v7x, 32 devices: a whole 2x2x4 slice. The times are simulated.
32 devices in a mesh: dp: 16 (over z, x, core), rep: 2 (over y).
Axes of the slice: x: 2, y: 2, z: 4, core: 2. Of those that a mesh axis runs over, the one named last changes fastest.
Arguments:
- tokens: bfloat16 [32, 1024, 768], P(('dp', 'rep')), may hold values from -6 to 6
- segment_ids: int32 [32, 1024], P(('dp', 'rep')), may hold values from 0 to 3, never falling along the last dimension, each value on 1 to 512 neighbouring positions
- cotangent: bfloat16 [32, 1024, 768], P(('dp', 'rep')), may hold values from -6 to 6
- w_qkv: float32 [768, 2304], P('dp'), may hold values from -0.21875 to 0.21875
- w_out: float32 [768, 768], P('dp'), may hold values from -0.875 to 0.875
- w_up: float32 [768, 3072], P('dp'), may hold values from -0.21875 to 0.21875
- w_down: float32 [3072, 768], P('dp'), may hold values from -0.109375 to 0.109375
- small_params: float32 [12, 768], P(None, 'dp'), may hold values from -0.35 to 1.5, as said below
- mom1_qkv: float32 [768, 2304], P('dp'), may hold values from -320 to 320
- mom1_out: float32 [768, 768], P('dp'), may hold values from -224 to 224
- mom1_up: float32 [768, 3072], P('dp'), may hold values from -320 to 320
- mom1_down: float32 [3072, 768], P('dp'), may hold values from -640 to 640
- mom1_small: float32 [12, 768], P(None, 'dp'), may hold values from -512 to 512
- mom2_qkv: float32 [768, 2304], P('dp'), may hold values from 1474.56 to 23592.96
- mom2_out: float32 [768, 768], P('dp'), may hold values from 655.36 to 10485.76
- mom2_up: float32 [768, 3072], P('dp'), may hold values from 1474.56 to 23592.96
- mom2_down: float32 [3072, 768], P('dp'), may hold values from 5898.24 to 94371.84
- mom2_small: float32 [12, 768], P(None, 'dp'), may hold values from 4096 to 65536
Outputs:
- out_tokens: bfloat16 [32, 1024, 768], P(('dp', 'rep'))
- grad_tokens: bfloat16 [32, 1024, 768], P(('dp', 'rep'))
- new_qkv: float32 [768, 2304], P('dp')
- new_out: float32 [768, 768], P('dp')
- new_up: float32 [768, 3072], P('dp')
- new_down: float32 [3072, 768], P('dp')
- new_small: float32 [12, 768], P(None, 'dp')
- next1_qkv: float32 [768, 2304], P('dp')
- next1_out: float32 [768, 768], P('dp')
- next1_up: float32 [768, 3072], P('dp')
- next1_down: float32 [3072, 768], P('dp')
- next1_small: float32 [12, 768], P(None, 'dp')
- next2_qkv: float32 [768, 2304], P('dp')
- next2_out: float32 [768, 768], P('dp')
- next2_up: float32 [768, 3072], P('dp')
- next2_down: float32 [3072, 768], P('dp')
- next2_small: float32 [12, 768], P(None, 'dp')
Inputs may be any that keep to these rules, and one draw needn't show every extreme that they name: `segment_ids`: each row holds 4 documents in order, each 1 to 512 tokens long, one exactly that long. `small_params`: gains lie in 0.5 to 1.5, biases in -0.35 to 0.35.
All inputs are finite; a program needn't handle non-finite values.
Results may differ from a plain program's by a relative error of at most 0.019.
Values may be sent and summed in bfloat16 or wider, within the bound.
No kernel may reach another device: no remote copies, remote signals or barrier semaphores. Data moves between devices by JAX's collectives and lax.ppermute only.
A program may use at most 192 MiB of HBM per device.

v0:
```python
import math

import jax
import jax.numpy as jnp
from jax import lax
from jax.sharding import PartitionSpec as P

HEADS = 12
STEP = 10


BETA1 = 0.5
BETA2 = 0.5
ADAM_EPS = 1e-08
DECAY = 0.05
RATES = (0.04, 0.15, 0.04, 0.02, 0.3)


def layer_norm(value, gain, bias):
    center = value - jnp.mean(value, -1, keepdims=True)
    spread = jnp.mean(center * center, -1, keepdims=True)
    return center * lax.rsqrt(spread + 1e-06) * gain + bias


def mask_softmax(scores, same):
    masked = jnp.where(same, scores, -1000000000.0)
    shifted = jnp.exp(masked - jnp.max(masked, -1, keepdims=True))
    return shifted / jnp.sum(shifted, -1, keepdims=True)


def gelu_tanh(value):
    return jax.nn.gelu(value, approximate=True)


def inner_rows(left, right):
    return lax.dot_general(
        left, right, (((0,), (0,)), ((), ())), preferred_element_type=jnp.float32
    )


def outer_rows(left, right):
    return lax.dot_general(
        left, right, (((1,), (1,)), ((), ())), preferred_element_type=jnp.float32
    )


def adamw(weight, grad, mom_one, mom_two, rate):
    next_one = BETA1 * mom_one + (1.0 - BETA1) * grad
    next_two = BETA2 * mom_two + (1.0 - BETA2) * grad * grad
    fixed_one = next_one / (1.0 - BETA1**STEP)
    fixed_two = next_two / (1.0 - BETA2**STEP)
    updated = weight - rate * (fixed_one / (jnp.sqrt(fixed_two) + ADAM_EPS) + DECAY * weight)
    return (updated, next_one, next_two)


def shards(
    tokens,
    segment_ids,
    cotangent,
    w_qkv,
    w_out,
    w_up,
    w_down,
    small_params,
    mom1_qkv,
    mom1_out,
    mom1_up,
    mom1_down,
    mom1_small,
    mom2_qkv,
    mom2_out,
    mom2_up,
    mom2_down,
    mom2_small,
):
    bf16 = jnp.bfloat16
    f32 = jnp.float32
    model_width = tokens.shape[2]
    row_count = tokens.shape[1]
    head_size = model_width // HEADS
    score_scale = 1.0 / math.sqrt(head_size)
    inputs = tokens[0].astype(f32)
    segment_row = segment_ids[0]
    same = segment_row[:, None] == segment_row[None, :]
    fetched = (
        lax.all_gather(w_qkv.astype(bf16), "dp", axis=0, tiled=True),
        lax.all_gather(w_out.astype(bf16), "dp", axis=0, tiled=True),
        lax.all_gather(w_up.astype(bf16), "dp", axis=0, tiled=True),
        lax.all_gather(w_down.astype(bf16), "dp", axis=0, tiled=True),
        lax.all_gather(small_params.astype(bf16), "dp", axis=1, tiled=True),
    )
    full_qkv, full_out, full_up, full_down, full_small = fetched
    smalls = full_small.astype(f32)
    pieces = [smalls[place] for place in range(8)]
    gain_one, bias_one, query_bias, value_bias, out_bias, gain_two, bias_two, down_bias = pieces
    up_bias = smalls[8:].reshape(-1)
    norm_one, pull_one = jax.vjp(layer_norm, inputs, gain_one, bias_one)
    normed = norm_one.astype(bf16)
    projected = jnp.dot(normed, full_qkv, preferred_element_type=f32)
    queries = (projected[:, :model_width] + query_bias).astype(bf16)
    keys_all = projected[:, model_width : 2 * model_width].astype(bf16)
    vals_all = (projected[:, 2 * model_width :] + value_bias).astype(bf16)

    def split_heads(value):
        return value.reshape(row_count, HEADS, head_size).transpose(1, 0, 2)

    def merge_heads(value):
        return value.transpose(1, 0, 2).reshape(row_count, model_width)

    head_q, head_k, head_v = (split_heads(queries), split_heads(keys_all), split_heads(vals_all))

    def head_forward(head_inputs):
        part_q, part_k, part_v = head_inputs
        scores = outer_rows(part_q, part_k) * score_scale
        probs = mask_softmax(scores, same).astype(bf16)
        return jnp.dot(probs, part_v, preferred_element_type=f32)

    mixed = merge_heads(lax.map(head_forward, (head_q, head_k, head_v))).astype(bf16)
    after_attn = inputs + jnp.dot(mixed, full_out, preferred_element_type=f32) + out_bias
    norm_two, pull_two = jax.vjp(layer_norm, after_attn, gain_two, bias_two)
    normed_two = norm_two.astype(bf16)
    pre_act = jnp.dot(normed_two, full_up, preferred_element_type=f32) + up_bias
    hidden_f, pull_gelu = jax.vjp(gelu_tanh, pre_act)
    hidden = hidden_f.astype(bf16)
    result = after_attn + jnp.dot(hidden, full_down, preferred_element_type=f32) + down_bias
    again = (
        lax.all_gather(w_qkv.astype(bf16), "dp", axis=0, tiled=True),
        lax.all_gather(w_out.astype(bf16), "dp", axis=0, tiled=True),
        lax.all_gather(w_up.astype(bf16), "dp", axis=0, tiled=True),
        lax.all_gather(w_down.astype(bf16), "dp", axis=0, tiled=True),
    )
    back_qkv, back_out, back_up, back_down = again
    out_grad = cotangent[0].astype(f32)
    grad_down_bias = jnp.sum(out_grad, 0)
    out_low = out_grad.astype(bf16)
    grad_down = inner_rows(hidden, out_low)
    grad_hidden = outer_rows(out_low, back_down)
    grad_pre = pull_gelu(grad_hidden)[0]
    grad_up_bias = jnp.sum(grad_pre, 0)
    pre_low = grad_pre.astype(bf16)
    grad_up = inner_rows(normed_two, pre_low)
    grad_norm_two = outer_rows(pre_low, back_up)
    grad_after, grad_gain_two, grad_bias_two = pull_two(grad_norm_two)
    grad_after = out_grad + grad_after
    grad_out_bias = jnp.sum(grad_after, 0)
    after_low = grad_after.astype(bf16)
    grad_out = inner_rows(mixed, after_low)
    grad_mixed = outer_rows(after_low, back_out).astype(bf16)

    def head_backward(head_inputs):
        part_q, part_k, part_v, part_d = head_inputs
        scores = outer_rows(part_q, part_k) * score_scale
        probs, pull_soft = jax.vjp(lambda values: mask_softmax(values, same), scores)
        grad_vals = inner_rows(probs.astype(bf16), part_d)
        grad_probs = outer_rows(part_d, part_v)
        grad_scores = pull_soft(grad_probs)[0].astype(bf16)
        grad_q = jnp.dot(grad_scores, part_k, preferred_element_type=f32) * score_scale
        grad_k = inner_rows(grad_scores, part_q) * score_scale
        return (grad_q, grad_k, grad_vals)

    grads_q, grads_k, grads_v = lax.map(
        head_backward, (head_q, head_k, head_v, split_heads(grad_mixed))
    )
    low_q = merge_heads(grads_q).astype(bf16)
    low_k = merge_heads(grads_k).astype(bf16)
    low_v = merge_heads(grads_v).astype(bf16)
    grad_query_bias = jnp.sum(low_q.astype(f32), 0)
    grad_value_bias = jnp.sum(low_v.astype(f32), 0)
    grad_proj = jnp.concatenate([low_q, low_k, low_v], 1)
    grad_qkv = inner_rows(normed, grad_proj)
    grad_norm_one = outer_rows(grad_proj, back_qkv)
    grad_inputs, grad_gain_one, grad_bias_one = pull_one(grad_norm_one)
    grad_inputs = grad_after + grad_inputs
    stacked = jnp.stack(
        [
            grad_gain_one,
            grad_bias_one,
            grad_query_bias,
            grad_value_bias,
            grad_out_bias,
            grad_gain_two,
            grad_bias_two,
            grad_down_bias,
        ]
    )
    grad_small = jnp.concatenate([stacked, grad_up_bias.reshape(-1, model_width)], 0)
    partial_value = (
        lax.psum_scatter(grad_qkv, "dp", scatter_dimension=0, tiled=True),
        lax.psum_scatter(grad_out, "dp", scatter_dimension=0, tiled=True),
        lax.psum_scatter(grad_up, "dp", scatter_dimension=0, tiled=True),
        lax.psum_scatter(grad_down, "dp", scatter_dimension=0, tiled=True),
        lax.psum_scatter(grad_small, "dp", scatter_dimension=1, tiled=True),
    )
    owned = (
        lax.psum(partial_value[0].astype(jnp.bfloat16), "rep").astype(jnp.float32),
        lax.psum(partial_value[1].astype(jnp.bfloat16), "rep").astype(jnp.float32),
        lax.psum(partial_value[2].astype(jnp.bfloat16), "rep").astype(jnp.float32),
        lax.psum(partial_value[3].astype(jnp.bfloat16), "rep").astype(jnp.float32),
        lax.psum(partial_value[4].astype(jnp.bfloat16), "rep").astype(jnp.float32),
    )
    masters = (w_qkv, w_out, w_up, w_down, small_params)
    firsts = (mom1_qkv, mom1_out, mom1_up, mom1_down, mom1_small)
    seconds = (mom2_qkv, mom2_out, mom2_up, mom2_down, mom2_small)
    updates = [
        adamw(masters[place], owned[place], firsts[place], seconds[place], RATES[place])
        for place in range(5)
    ]
    return (
        result[None].astype(bf16),
        grad_inputs[None].astype(bf16),
        updates[0][0],
        updates[1][0],
        updates[2][0],
        updates[3][0],
        updates[4][0],
        updates[0][1],
        updates[1][1],
        updates[2][1],
        updates[3][1],
        updates[4][1],
        updates[0][2],
        updates[1][2],
        updates[2][2],
        updates[3][2],
        updates[4][2],
    )


def solution(mesh):
    return jax.shard_map(
        shards,
        mesh=mesh,
        in_specs=(
            P(("dp", "rep"), None, None),
            P(("dp", "rep"), None),
            P(("dp", "rep"), None, None),
            P("dp", None),
            P("dp", None),
            P("dp", None),
            P("dp", None),
            P(None, "dp"),
            P("dp", None),
            P("dp", None),
            P("dp", None),
            P("dp", None),
            P(None, "dp"),
            P("dp", None),
            P("dp", None),
            P("dp", None),
            P("dp", None),
            P(None, "dp"),
        ),
        out_specs=(
            P(("dp", "rep"), None, None),
            P(("dp", "rep"), None, None),
            P("dp", None),
            P("dp", None),
            P("dp", None),
            P("dp", None),
            P(None, "dp"),
            P("dp", None),
            P("dp", None),
            P("dp", None),
            P("dp", None),
            P(None, "dp"),
            P("dp", None),
            P("dp", None),
            P("dp", None),
            P("dp", None),
            P(None, "dp"),
        ),
        check_vma=False,
    )
```

profile of v0, /device:TPU:0, one launch (start us, length us, event | category | flops | bytes accessed | tf_op | source)
XLA Modules:
  0.0 891.8 jit_solution(10355606284952386695)
XLA Ops:
  14.6 23.3 %all-gather = bf16[16,48,12]{1,2,0:T(8,128)(2,1)S(1)} all-gather(bf16[1,48,12]{1,2,0:T(8,128)(2,1)S(1)} %convert_bitcast_fusion.1), channel_id=1, replica_groups=mesh['dp'=16,'rep'=2] {'dp'}, dimensions={0}, use_global_device_ids=true | all-gather | bytes 19584 | tf_op jit(solution)/shard_map/all_gather | solution.py:90
  42.5 18.1 %all-gather.6.cloned.1.call-done = bf16[768,2304]{1,0:T(8,128)(2,1)} async-done(((bf16[48,2304]{1,0:T(8,128)(2,1)}), bf16[768,2304]{1,0:T(8,128)(2,1)}) %all-gather.6.cloned.1.call-update) | async-done | bytes 3538960 | tf_op jit(solution)/shard_map/all_gather | solution.py:86
  60.6 6.3 fusion.96
  75.7 4.1 copy.94
  79.8 4.2 copy.95
  86.5 4.1 copy.93
  92.0 69.3 %while.26 = (s32[]{:T(128)}, bf16[12,1024,64]{1,2,0:T(8,128)(2,1)}, bf16[12,1024,64]{2,1,0:T(8,128)(2,1)}, bf16[12,1024,64]{2,1,0:T(8,128)(2,1)}, bf16[12,1024,6...) while((s32[]{:T(128)}, bf16[12,1024,64]{1,2,0:T(8,128)(2,1)}, ...), condition=%wide.region_5.6_spmd.clone, body=%wide.region_2.5_spmd.clone.sunk | while | flops 284162048 | bytes 13674581 | solution.py:118
  129.4 3.0 fusion.145
  146.7 3.0 fusion.145
  161.4 3.4 fusion.106
  166.8 11.1 %fusion.98 = f32[1024,3072]{1,0:T(8,128)} fusion(bf16[768,3072]{1,0:T(8,128)(2,1)} %all-gather.10.cloned.1.call-done, f32[1024,768]{0,1:T(8,128)} %copy-done, f32[768]{0:T(1024)S(1)} %get-tuple-element.259, f32[768]{0:T(1024)S(1)} %get-tuple-element.257, f32[1024]{0:T(1024)S(1)} %fusion.92, f32[1024]{0:T(1024)S(1)} %broadcast_multiply_fusion), kind=kOutput, calls=%fused_computation.164 | convolution fusion | flops 4835770368 | bytes 20461568 | tf_op jit(solution)/shard_map/dot_general | solution.py:122
  177.9 32.7 %all-gather.12.cloned.1.call-done = bf16[3072,768]{1,0:T(8,128)(2,1)} async-done(((bf16[192,768]{1,0:T(8,128)(2,1)}), bf16[3072,768]{1,0:T(8,128)(2,1)}) %all-gather.12.cloned.1.call-update) | async-done | bytes 4718608 | tf_op jit(solution)/shard_map/all_gather | solution.py:89
  210.6 17.4 %fusion.109 = (f32[3072]{0:T(1024)}, bf16[1024,3072]{1,0:T(8,128)(2,1)S(1)}) fusion(f32[1024,3072]{1,0:T(8,128)} %fusion.98, f32[3072]{0:T(1024)S(1)} %add.228, bf16[3072,768]{1,0:T(8,128)(2,1)} %all-gather.12.cloned.1.call-done, bf16[1,1024,768]{2,1,0:T(8,128)(2,1)} %param.24), kind=kOutput, calls=%fused_computation.170 | convolution fusion | flops 4901041152 | bytes 25190400 | tf_op jit(solution)/shard_map/dot_general | solution.py:42
  227.9 6.8 fusion.108
  234.7 3.5 copy.98
  238.2 3.9 multiply_reduce_fusion.1
  249.5 4.3 convolution_convert_fusion
  253.8 4.3 copy.99
  262.2 186.8 %while.27 = (s32[]{:T(128)}, bf16[12,1024,64]{1,2,0:T(8,128)(2,1)}, bf16[12,1024,64]{1,2,0:T(8,128)(2,1)}, bf16[12,1024,64]{1,2,0:T(8,128)(2,1)}, bf16[12,1024,6...) while((s32[]{:T(128)}, bf16[12,1024,64]{1,2,0:T(8,128)(2,1)}, ...), condition=%wide.region_16.17_spmd.clone, body=%wide.region_10.16_spmd.clone.sunk | while | flops 702676992 | bytes 48874604 | solution.py:161
  449.0 9.3 %fusion.76 = f32[768,2304]{1,0:T(8,128)} fusion(bf16[1024,768]{0,1:T(8,128)(2,1)} %bitcast.196, bf16[1024,768]{0,1:T(8,128)(2,1)} %bitcast.204, bf16[1024,768]{0,1:T(8,128)(2,1)} %bitcast.198, bf16[1,1024,768]{1,2,0:T(8,128)(2,1)S(1)} %copy.88, f32[768]{0:T(1024)S(1)} %copy-done.42, f32[768]{0:T(1024)S(1)} %copy-done.30, f32[1024]{0:T(1024)S(1)} %copy-done.32, ...), kind=kOutput, calls=%fused_computation.110 | convolution fusion | flops 3642753024 | bytes 13383680 | tf_op jit(solution)/shard_map/dot_general | solution.py:36
  458.4 13.5 %fusion.79 = f32[3072,768]{1,0:T(8,128)} fusion(bf16[1,1024,768]{2,1,0:T(8,128)(2,1)} %param.24, f32[1024,3072]{1,0:T(8,128)} %fusion.98, f32[3072]{0:T(1024)S(1)} %add.228), kind=kOutput, calls=%fused_computation.114 | convolution fusion | flops 4863295488 | bytes 23605248 | tf_op jit(solution)/shard_map/dot_general | solution.py:36
  472.6 11.0 %fusion.72 = f32[768,3072]{1,0:T(8,128)} fusion(bf16[1024,3072]{1,0:T(8,128)(2,1)} %copy-done.43, f32[1024,768]{0,1:T(8,128)} %copy-done, f32[768]{0:T(1024)S(1)} %copy-done.22, f32[768]{0:T(1024)S(1)} %get-tuple-element.257, f32[1024]{0:T(1024)S(1)} %fusion.92, f32[1024]{0:T(1024)S(1)} %broadcast_multiply_fusion), kind=kOutput, calls=%fused_computation.103 | convolution fusion | flops 4835770368 | bytes 18888704 | tf_op jit(solution)/shard_map/dot_general | solution.py:36
  484.3 9.2 %fusion.107 = (f32[768]{0:T(1024)S(1)}, f32[1024,768]{1,0:T(8,128)}) fusion(bf16[768,2304]{1,0:T(8,128)(2,1)} %all-gather.6.cloned.1.call-done, bf16[1024,768]{0,1:T(8,128)(2,1)} %bitcast.197, bf16[1024,768]{0,1:T(8,128)(2,1)} %bitcast.205, bf16[1024,768]{0,1:T(8,128)(2,1)} %bitcast.199), kind=kOutput, calls=%fused_computation.168 | convolution fusion | flops 3638820096 | bytes 11406336 | tf_op jit(solution)/shard_map/dot_general | solution.py:42
  494.1 3.8 copy.103
  502.5 3.2 convert_reduce_fusion.1
  508.4 38.7 %reduce-scatter.8.cloned.1.call-done = f32[48,2304]{1,0:T(8,128)} async-done(((f32[768,2304]{1,0:T(8,128)}), f32[48,2304]{1,0:T(8,128)}) %reduce-scatter.8.cloned.1.call-update) | async-done | bytes 442384 | tf_op jit(solution)/shard_map/reduce_scatter | solution.py:188
  548.8 113.3 %reduce-scatter.14.cloned.1.call-done = f32[192,768]{1,0:T(8,128)} async-done(((f32[3072,768]{1,0:T(8,128)}), f32[192,768]{1,0:T(8,128)}) %reduce-scatter.14.cloned.1.call-update) | async-done | bytes 589840 | tf_op jit(solution)/shard_map/reduce_scatter | solution.py:191
  663.9 114.0 %reduce-scatter.12.cloned.1.call-done = f32[48,3072]{1,0:T(8,128)} async-done(((f32[768,3072]{1,0:T(8,128)}), f32[48,3072]{1,0:T(8,128)}) %reduce-scatter.12.cloned.1.call-update) | async-done | bytes 589840 | tf_op jit(solution)/shard_map/reduce_scatter | solution.py:190
  779.7 11.3 %fusion.82 = bf16[1,1024,768]{1,2,0:T(8,128)(2,1)S(1)} fusion(f32[768]{0:T(1024)S(1)} %copy-done.40, f32[1024,768]{0,1:T(8,128)} %copy-done, bf16[3072,768]{1,0:T(8,128)(2,1)} %all-gather.12.cloned.1.call-done, f32[1024,3072]{1,0:T(8,128)} %fusion.98, f32[3072]{0:T(1024)S(1)} %add.228), kind=kOutput, calls=%fused_computation.117 | convolution fusion | flops 4865654784 | bytes 22035456 | tf_op jit(solution)/shard_map/dot_general | solution.py:125
  794.2 43.1 %reduce-scatter.16.cloned.1.call-done = f32[48,12]{1,0:T(8,128)} async-done(((f32[768,12]{1,0:T(8,128)}), f32[48,12]{1,0:T(8,128)}) %reduce-scatter.16.cloned.1.call-update) | async-done | bytes 2320
  838.1 4.9 psum.39
  843.7 33.3 %all-reduce.3.cloned.1.call-done = (bf16[48,2304]{1,0:T(8,128)(2,1)}, bf16[48,768]{1,0:T(8,128)(2,1)}, bf16[48,3072]{1,0:T(8,128)(2,1)}, bf16[192,768]{1,0:T(8,128)(2,1)}) async-done(((bf16[48,2304]{1,0:T(8,128)(2,1)}, bf16[48,768]{1,0:T(8,128)(2,1)}, bf16[48,3072]{1,0:T(8,128)(2,1)}, bf16[192,768]{1,0:T(8,128)(2,1)}), (bf16[48,2304]{1,0:T(8,128)(2,1)}, bf16[48,768]{1,0:T(8,128)(2,1)}, ...) | async-done | bytes 884752 | tf_op jit(solution)/shard_map/psum | solution.py:195
  (338 shorter events, 313.9 us)
Async XLA Ops:
  7.2 31.4 %copy-start.13 = (bf16[1,1024,768]{2,1,0:T(8,128)(2,1)S(1)}, bf16[1,1024,768]{2,1,0:T(8,128)(2,1)}, u32[]{:S(2)}) copy-start(bf16[1,1024,768]{2,1,0:T(8,128)(2,1)} %param.22) | copy-start | bytes 4718596
  7.2 53.4 %all-gather.6.cloned.1.call-start = ((), (), s32[]{:S(2)}) async-start(), calls=%async_computation.5 | async-start | bytes 3760128 | tf_op jit(solution)/shard_map/all_gather | solution.py:86
  9.1 152.2 %all-gather.8.cloned.1.call-start = ((), (), s32[]{:S(2)}) async-start(), calls=%async_computation.6 | async-start | bytes 1253376 | tf_op jit(solution)/shard_map/all_gather | solution.py:87
  10.7 156.1 %all-gather.10.cloned.1.call-start = ((), (), s32[]{:S(2)}) async-start(), calls=%async_computation.7 | async-start | bytes 5013504 | tf_op jit(solution)/shard_map/all_gather | solution.py:88
  12.6 198.0 %all-gather.12.cloned.1.call-start = ((), (), s32[]{:S(2)}) async-start(), calls=%async_computation.8 | async-start | bytes 5013504 | tf_op jit(solution)/shard_map/all_gather | solution.py:89
  14.5 492.3 %reduce-scatter.10.cloned.1.call-start = ((), (), s32[]{:S(2)}) async-start(), calls=%async_computation.10 | async-start | bytes 2506752 | tf_op jit(solution)/shard_map/reduce_scatter | solution.py:189
  38.6 22.0 %copy-start.29 = (f32[768]{0:T(1024)}, f32[768]{0:T(1024)S(1)}, u32[]{:S(2)}) copy-start(f32[768]{0:T(1024)S(1)} %get-tuple-element.264) | copy-start | bytes 9220
  38.6 22.0 %copy-start.41 = (f32[768]{0:T(1024)}, f32[768]{0:T(1024)S(1)}, u32[]{:S(2)}) copy-start(f32[768]{0:T(1024)S(1)} %get-tuple-element.263) | copy-start | bytes 9220
  38.6 128.2 %copy-start.21 = (f32[768]{0:T(1024)}, f32[768]{0:T(1024)S(1)}, u32[]{:S(2)}) copy-start(f32[768]{0:T(1024)S(1)} %get-tuple-element.259) | copy-start | bytes 9220
  39.7 27.2 %copy-start.27 = (f32[1024]{0:T(1024)}, f32[1024]{0:T(1024)S(1)}, u32[]{:S(2)}) copy-start(f32[1024]{0:T(1024)S(1)} %broadcast_multiply_fusion.1) | copy-start | bytes 12292
  40.7 26.1 %copy-start.31 = (f32[1024]{0:T(1024)}, f32[1024]{0:T(1024)S(1)}, u32[]{:S(2)}) copy-start(f32[1024]{0:T(1024)S(1)} %fusion.91) | copy-start | bytes 12292
  210.6 17.4 %copy-start.9 = (bf16[768,3072]{1,0:T(8,128)(2,1)S(1)}, bf16[768,3072]{1,0:T(8,128)(2,1)}, u32[]{:S(2)}) copy-start(bf16[768,3072]{1,0:T(8,128)(2,1)} %all-gather.10.cloned.1.call-done) | copy-start | bytes 14155780
  249.5 297.6 %reduce-scatter.8.cloned.1.call-start = ((), (), s32[]{:S(2)}) async-start(), calls=%async_computation.9 | async-start | bytes 7520256 | tf_op jit(solution)/shard_map/reduce_scatter | solution.py:188
  262.2 186.8 %copy-start.28 = (f32[1024]{0:T(1024)S(1)}, f32[1024]{0:T(1024)}, u32[]{:S(2)}) copy-start(f32[1024]{0:T(1024)} %copy-done.27) | copy-start | bytes 12292
  262.2 186.8 %copy-start.30 = (f32[768]{0:T(1024)S(1)}, f32[768]{0:T(1024)}, u32[]{:S(2)}) copy-start(f32[768]{0:T(1024)} %copy-done.29) | copy-start | bytes 9220
  262.2 186.8 %copy-start.32 = (f32[1024]{0:T(1024)S(1)}, f32[1024]{0:T(1024)}, u32[]{:S(2)}) copy-start(f32[1024]{0:T(1024)} %copy-done.31) | copy-start | bytes 12292
  262.2 186.8 %copy-start.42 = (f32[768]{0:T(1024)S(1)}, f32[768]{0:T(1024)}, u32[]{:S(2)}) copy-start(f32[768]{0:T(1024)} %copy-done.41) | copy-start | bytes 9220
  458.3 203.8 %reduce-scatter.14.cloned.1.call-start = ((), (), s32[]{:S(2)}) async-start(), calls=%async_computation.12 | async-start | bytes 10027008 | tf_op jit(solution)/shard_map/reduce_scatter | solution.py:191
  471.9 305.9 %reduce-scatter.12.cloned.1.call-start = ((), (), s32[]{:S(2)}) async-start(), calls=%async_computation.11 | async-start | bytes 10027008 | tf_op jit(solution)/shard_map/reduce_scatter | solution.py:190
  483.6 353.7 %reduce-scatter.16.cloned.1.call-start = ((), (), s32[]{:S(2)}) async-start(), calls=%async_computation.13 | async-start | bytes 417792
  484.3 9.2 %copy-start.6 = (bf16[12,1024,64]{1,2,0:T(8,128)(2,1)S(1)}, bf16[12,1024,64]{1,2,0:T(8,128)(2,1)}, u32[]{:S(2)}) copy-start(bf16[12,1024,64]{1,2,0:T(8,128)(2,1)} %get-tuple-element.101) | copy-start | bytes 4718596
  505.7 274.0 %copy-start.40 = (f32[768]{0:T(1024)S(1)}, f32[768]{0:T(1024)}, u32[]{:S(2)}) copy-start(f32[768]{0:T(1024)} %get-tuple-element.258) | copy-start | bytes 9220
  506.8 370.3 %all-reduce.3.cloned.1.call-start = ((), (), s32[]{:S(2)}) async-start(), calls=%async_computation.14 | async-start | bytes 1769472 | tf_op jit(solution)/shard_map/psum | solution.py:195
  791.0 52.1 %copy-start.36 = (f32[12,48]{1,0:T(8,128)S(1)}, f32[12,48]{1,0:T(8,128)}, u32[]{:S(2)}) copy-start(f32[12,48]{1,0:T(8,128)} %param.29) | copy-start | bytes 6916
  791.0 52.1 %copy-start.38 = (f32[12,48]{1,0:T(8,128)S(1)}, f32[12,48]{1,0:T(8,128)}, u32[]{:S(2)}) copy-start(f32[12,48]{1,0:T(8,128)} %param.34) | copy-start | bytes 6916
  791.0 52.0 %copy-start.39 = (f32[12,48]{1,0:T(8,128)S(1)}, f32[12,48]{1,0:T(8,128)}, u32[]{:S(2)}) copy-start(f32[12,48]{1,0:T(8,128)} %param.39) | copy-start | bytes 6916
  791.0 86.0 %copy-start.16 = (f32[48,768]{1,0:T(8,128)S(1)}, f32[48,768]{1,0:T(8,128)}, u32[]{:S(2)}) copy-start(f32[48,768]{1,0:T(8,128)} %param.26) | copy-start | bytes 442372
  791.0 86.0 %copy-start.25 = (f32[48,768]{1,0:T(8,128)S(1)}, f32[48,768]{1,0:T(8,128)}, u32[]{:S(2)}) copy-start(f32[48,768]{1,0:T(8,128)} %param.31) | copy-start | bytes 442372
  792.6 84.4 %copy-start.26 = (f32[48,768]{1,0:T(8,128)S(1)}, f32[48,768]{1,0:T(8,128)}, u32[]{:S(2)}) copy-start(f32[48,768]{1,0:T(8,128)} %param.36) | copy-start | bytes 442372
  792.6 89.0 %copy-start.10 = (f32[48,3072]{1,0:T(8,128)S(1)}, f32[48,3072]{1,0:T(8,128)}, u32[]{:S(2)}) copy-start(f32[48,3072]{1,0:T(8,128)} %param.27) | copy-start | bytes 1769476
  794.2 87.4 %copy-start.17 = (f32[48,3072]{1,0:T(8,128)S(1)}, f32[48,3072]{1,0:T(8,128)}, u32[]{:S(2)}) copy-start(f32[48,3072]{1,0:T(8,128)} %param.32) | copy-start | bytes 1769476
  794.2 87.4 %copy-start.18 = (f32[48,3072]{1,0:T(8,128)S(1)}, f32[48,3072]{1,0:T(8,128)}, u32[]{:S(2)}) copy-start(f32[48,3072]{1,0:T(8,128)} %param.37) | copy-start | bytes 1769476
  (22 other events, 77.4 us)
Sparse Core Ops, SparseCore 0:
  10.9 49.6 all-gather.5
  63.4 37.3 all-gather.7
  103.7 52.3 all-gather.9
  158.8 51.7 all-gather.11
  249.6 61.4 reduce-scatter.9
  458.4 88.5 reduce-scatter.7
  551.2 110.8 reduce-scatter.13
  666.7 111.0 reduce-scatter.11
  781.9 55.3 reduce-scatter.15
  840.9 36.0 all-reduce.2
where the time goes:
time: 904 us; the launch traced here: 892 us
  waiting for transfers between devices  393 us (43%)
  matrix products  292 us (32%)
  other arithmetic  108 us (12%)
  local copies, waits for them, and re-layouts  53.9 us (6%)
  blocking collectives  28.2 us (3%)
  between operations  15.1 us (2%)
    reduce_scatter x1, waiting for transfers between devices, shards(): lax.psum_scatter(grad_up, 'dp', scatter_dimension=0, tiled=True)  114 us
    reduce_scatter x1, waiting for transfers between devices, shards(): lax.psum_scatter(grad_down, 'dp', scatter_dimension=0, tiled=True)  113 us
    dot_general x40, matrix products, outer_rows(): lax.dot_general(left, right, (((1,), (1,)), ((), ())), preferred_element_...  104 us
    dot_general x28, matrix products, inner_rows(): lax.dot_general(left, right, (((0,), (0,)), ((), ())), preferred_element_...  95.1 us
    unnamed x11, waiting for transfers between devices  43.3 us
    reduce_scatter x1, waiting for transfers between devices, shards(): lax.psum_scatter(grad_qkv, 'dp', scatter_dimension=0, tiled=True)  38.7 us
    dot_general x12, matrix products, head_forward(): return jnp.dot(probs, part_v, preferred_element_type=f32)  35.5 us
    psum x1, waiting for transfers between devices, shards(): lax.psum(partial_value[0].astype(jnp.bfloat16), 'rep').astype(jnp.float32)  33.3 us
  transfers between devices with their start and end apart: 10, of which 7 were waited for; matrix products, arithmetic and copies ran while one was open for 45% of the time, Pallas kernels for 0%

commit v1 on v0

v1 whole, which is shorter than its diff:
```python
import functools
import math

import jax
import jax.numpy as jnp
from jax import lax
from jax.experimental import pallas as pl
from jax.experimental.pallas import tpu as pltpu
from jax.sharding import PartitionSpec as P

HEADS = 12
STEP = 10
BETA1 = 0.5
BETA2 = 0.5
ADAM_EPS = 1e-08
DECAY = 0.05
RATES = (0.04, 0.15, 0.04, 0.02, 0.3)

bf16 = jnp.bfloat16
f32 = jnp.float32

T = 1024
D = 768
FF = 3072
OWN = 16
RB = D // OWN
FB = FF // OWN // 3
FC = FF // 3
QR = 6 * RB
FR = 8 * RB + 6 * FB
SR = 16
B = 256
NB = T // B
MASK = 2.0**30
VMEM_LIMIT = 56 << 20

VM = pl.BlockSpec(memory_space=pltpu.VMEM)
SM = pl.BlockSpec(memory_space=pltpu.SMEM)


def params(**kw):
    return pltpu.CompilerParams(vmem_limit_bytes=VMEM_LIMIT, **kw)


def sds(shape, dtype):
    return jax.ShapeDtypeStruct(shape, dtype)


def cost(flops, nbytes, trans=0):
    return pl.CostEstimate(flops=int(flops), bytes_accessed=int(nbytes), transcendentals=int(trans))


def dot(a, b, ca, cb):
    return lax.dot_general(a, b, (((ca,), (cb,)), ((), ())), preferred_element_type=f32)


def fold(v):
    return jnp.sum(v.reshape(v.shape[0] // 8, 8, v.shape[1]), axis=0)


def rowsum(v):
    return jnp.sum(fold(v), axis=0, keepdims=True)


def gathered_rows(dst, refs, offs, base, tiles, rows, col):
    for s in range(OWN):
        ref, at = refs[s // 4], s % 4
        off = pl.multiple_of(offs[s] * rows, 16)
        for t in range(tiles):
            dst[pl.ds(off, rows), col + 128 * t : col + 128 * t + 128] = ref[
                at, base + t * rows : base + (t + 1) * rows, :
            ]


def scattered_rows(src, outs, offs, base, tiles, rows, col):
    for s in range(OWN):
        ref, at = outs[s // 8], s % 8
        off = pl.multiple_of(offs[s] * rows, 16)
        for t in range(tiles):
            ref[at, base + t * rows : base + (t + 1) * rows, :] = src[
                pl.ds(off, rows), col + 128 * t : col + 128 * t + 128
            ]


def pack_kernel(small, wq, wo, wu, wd, q0, q1, q2, o, f0, f1, f2):
    qs = (q0, q1, q2)
    fs = (f0, f1, f2)
    for g in range(3):
        for part in range(3):
            for t in range(2):
                c = D * part + 256 * g + 128 * t
                r = (2 * part + t) * RB
                qs[g][r : r + RB, :] = wq[:, c : c + 128].astype(bf16)
    q0[QR : QR + SR, :] = small[...].astype(bf16)
    for t in range(6):
        o[t * RB : (t + 1) * RB, :] = wo[:, 128 * t : 128 * t + 128].astype(bf16)
    for j in range(3):
        for t in range(8):
            a = wu[:, 384 * t + 64 * j : 384 * t + 64 * j + 64]
            b = wu[:, 384 * t + 192 + 64 * j : 384 * t + 192 + 64 * j + 64]
            fs[j][t * RB : (t + 1) * RB, :] = jnp.concatenate([a, b], axis=1).astype(bf16)
        for t in range(6):
            r = 8 * RB + t * FB
            fs[j][r : r + FB, :] = wd[FB * j : FB * j + FB, 128 * t : 128 * t + 128].astype(bf16)


def pack(small, wq, wo, wu, wd):
    small = jnp.pad(small, ((0, SR - small.shape[0]), (0, 128 - small.shape[1])))
    return pl.pallas_call(
        pack_kernel,
        out_shape=[sds((QR + SR, 128), bf16)]
        + [sds((QR, 128), bf16)] * 3
        + [sds((FR, 128), bf16)] * 3,
        in_specs=[VM] * 5,
        out_specs=[VM] * 7,
        compiler_params=params(),
        cost_estimate=cost(0, 6 << 20),
        name="pack",
    )(small, wq, wo, wu, wd)


def norm_kernel(offs, x, p0, p1, p2, p3, n1, n1t, small, *, base):
    @pl.when(pl.program_id(0) == 0)
    def _():
        acc = jnp.zeros((SR, D), f32)
        row = lax.broadcasted_iota(jnp.int32, (128, D), 0)
        col = lax.broadcasted_iota(jnp.int32, (128, D), 1)
        for s in range(OWN):
            ref = (p0, p1, p2, p3)[s // 4]
            hot = jnp.where((col == row + offs[s] * RB) & (row < RB), 1.0, 0.0).astype(bf16)
            acc += dot(ref[s % 4, base : base + SR, :], hot, 1, 0)
        small[...] = acc

    v = x[...].astype(f32)
    c = v - jnp.mean(v, -1, keepdims=True)
    r = lax.rsqrt(jnp.mean(c * c, -1, keepdims=True) + 1e-06)
    n = (c * r * small[0:1, :] + small[1:2, :]).astype(bf16)
    n1[...] = n
    n1t[...] = n.T


def norm_first(offs, x, pieces, base):
    whole = [pl.BlockSpec(p.shape, lambda r: (0, 0, 0)) for p in pieces]
    return pl.pallas_call(
        functools.partial(norm_kernel, base=base),
        grid=(NB,),
        out_shape=[sds((T, D), bf16), sds((D, T), bf16), sds((SR, D), f32)],
        in_specs=[SM, pl.BlockSpec((B, D), lambda r: (r, 0))] + whole,
        out_specs=[
            pl.BlockSpec((B, D), lambda r: (r, 0)),
            pl.BlockSpec((D, B), lambda r: (0, r)),
            pl.BlockSpec((SR, D), lambda r: (0, 0)),
        ],
        compiler_params=params(),
        cost_estimate=cost(1e7, 5 << 20),
        name="norm_first",
    )(offs, x, *pieces)


def segment_tail(segc, segr, minus):
    lane = lax.broadcasted_iota(jnp.int32, (T, 128), 1)
    left = jnp.where((segc[...] == lane) | ((lane >= 4) & (lane < 7)), 1.0, 0.0).astype(bf16)
    sub = lax.broadcasted_iota(jnp.int32, (16, T), 0)
    right = jnp.where((segr[...] != sub) & (sub < 4), -MASK, 0.0)
    return left, right


def three(v):
    hi = v.astype(bf16).astype(f32)
    rest = v - hi
    mid = rest.astype(bf16).astype(f32)
    return hi, mid, rest - mid


def attn_fwd_kernel(
    blk, offs, n1, p0, p1, p2, p3, small, segc, segr,
    q_o, k_o, v_o, mix_o, mixt_o, lse_o, w_o, kn, qt, vt, s_s, *, g,
):
    gathered_rows(w_o, (p0, p1, p2, p3), offs, 0, 6, RB, 0)
    qb = small[2:3, 256 * g : 256 * g + 256]
    vb = small[3:4, 256 * g : 256 * g + 256]
    q = (dot(n1[...], w_o[:, :256], 1, 0) + qb).astype(bf16)
    k = dot(n1[...], w_o[:, 256:512], 1, 0).astype(bf16)
    v = (dot(n1[...], w_o[:, 512:], 1, 0) + vb).astype(bf16)
    q_o[...] = q
    k_o[...] = k
    v_o[...] = v
    left, right = segment_tail(segc, segr, None)
    right = right.astype(bf16)
    qtt = (q * jnp.asarray(0.125, bf16)).T
    zero = jnp.zeros((64, T), bf16)
    pad = jnp.zeros((112, T), bf16)
    for p in range(2):
        kn[p, :, :128] = k[:, 128 * p : 128 * p + 128]
        kn[p, :, 128:] = left
        for e in range(2):
            h = 2 * p + e
            qt[h, 64 * e : 64 * e + 64, :] = qtt[64 * h : 64 * h + 64]
            qt[h, 64 - 64 * e : 128 - 64 * e, :] = zero
            qt[h, 128:144, :] = right
            qt[h, 144:, :] = pad
    vt[...] = v.T
    for i in range(NB):
        lo = blk[0, i]
        hi = blk[1, i]
        cols = slice(i * B, (i + 1) * B)

        def scores(j, tops):
            r = pl.ds(pl.multiple_of(j * B, B), B)
            out = []
            for h in range(4):
                s = dot(kn[h // 2, r, :], qt[h, :, cols], 1, 0)
                s_s[h, r, :] = s
                out.append(jnp.maximum(tops[h], jnp.max(s.reshape(B // 8, 8, B), axis=0)))
            return tuple(out)

        tops = lax.fori_loop(lo, hi, scores, tuple(jnp.full((8, B), -3e38, f32) for _ in range(4)))
        tops = [jnp.max(m, axis=0, keepdims=True) for m in tops]

        def mixing(j, carry):
            sums, accs = carry
            r = pl.ds(pl.multiple_of(j * B, B), B)
            new_sums, new_accs = [], []
            for h in range(4):
                e = jnp.exp(s_s[h, r, :] - tops[h])
                new_sums.append(sums[h] + fold(e))
                new_accs.append(accs[h] + dot(vt[64 * h : 64 * h + 64, r], e.astype(bf16), 1, 0))
            return tuple(new_sums), tuple(new_accs)

        zeros = (
            tuple(jnp.zeros((8, B), f32) for _ in range(4)),
            tuple(jnp.zeros((64, B), f32) for _ in range(4)),
        )
        sums, accs = lax.fori_loop(lo, hi, mixing, zeros)
        for h in range(4):
            total = jnp.sum(sums[h], axis=0, keepdims=True)
            mixt_o[64 * h : 64 * h + 64, cols] = (accs[h] / total).astype(bf16)
            lse_o[h : h + 1, cols] = tops[h] + jnp.log(total)
    mix_o[...] = mixt_o[...].T


def attn_fwd(g, blk, offs, n1, pieces, small, segc, segr):
    return pl.pallas_call(
        functools.partial(attn_fwd_kernel, g=g),
        out_shape=[sds((T, 256), bf16)] * 4
        + [sds((256, T), bf16), sds((4, T), f32), sds((D, D), bf16)],
        in_specs=[SM, SM] + [VM] * 8,
        out_specs=[VM] * 7,
        scratch_shapes=[
            pltpu.VMEM((2, T, 256), bf16),
            pltpu.VMEM((4, 256, T), bf16),
            pltpu.VMEM((256, T), bf16),
            pltpu.VMEM((4, T, B), f32),
        ],
        compiler_params=params(),
        cost_estimate=cost(9e9, 8 << 20, 4e6),
        name="attn_fwd",
    )(blk, offs, n1, *pieces, small, segc, segr)


def post_kernel(offs, x, m0, m1, m2, p0, p1, p2, p3, small, x1_o, n2_o, n2t_o, w):
    @pl.when(pl.program_id(0) == 0)
    def _():
        gathered_rows(w, (p0, p1, p2, p3), offs, 0, 6, RB, 0)

    a = x[...].astype(f32) + small[4:5, :]
    for g, m in enumerate((m0, m1, m2)):
        a += dot(m[...], w[256 * g : 256 * g + 256, :], 1, 0)
    x1_o[...] = a
    c = a - jnp.mean(a, -1, keepdims=True)
    r = lax.rsqrt(jnp.mean(c * c, -1, keepdims=True) + 1e-06)
    n = (c * r * small[5:6, :] + small[6:7, :]).astype(bf16)
    n2_o[...] = n
    n2t_o[...] = n.T


def post_attn(offs, x, mixes, pieces, small):
    rows = pl.BlockSpec((B, D), lambda r: (r, 0))
    part = pl.BlockSpec((B, 256), lambda r: (r, 0))
    return pl.pallas_call(
        post_kernel,
        grid=(NB,),
        out_shape=[sds((T, D), f32), sds((T, D), bf16), sds((D, T), bf16)],
        in_specs=[SM, rows, part, part, part]
        + [pl.BlockSpec(p.shape, lambda r: (0, 0, 0)) for p in pieces]
        + [pl.BlockSpec((SR, D), lambda r: (0, 0))],
        out_specs=[rows, rows, pl.BlockSpec((D, B), lambda r: (0, r))],
        scratch_shapes=[pltpu.VMEM((D, D), bf16)],
        compiler_params=params(),
        cost_estimate=cost(1.2e9, 10 << 20),
        name="post_attn",
    )(offs, x, *mixes, *pieces, small)


C0 = math.sqrt(2.0 / math.pi)
C1 = 0.044715


def ff_kernel(*refs, j, first):
    if first:
        offs, n2, n2t, dy, p0, p1, p2, p3, small = refs[:9]
        acc = None
        rest = refs[9:]
    else:
        offs, n2, n2t, dy, p0, p1, p2, p3, small, acc = refs[:10]
        rest = refs[10:]
    hid_o, acc_o, keep, send, wd, dub, wu, ub, n2ts, dys, ht, dp, gu, gd = rest
    step = pl.program_id(0)
    rows = pl.ds(pl.multiple_of(step * B, B), B)

    @pl.when(step == 0)
    def _():
        gathered_rows(wu, (p0, p1, p2, p3), offs, 0, 8, RB, 0)
        gathered_rows(wd, (p0, p1, p2, p3), offs, 8 * RB, 6, FB, 0)
        for t in range(8):
            halves = []
            for d in (2 * t, 2 * t + 1):
                c = 192 * (d % 4) + FB * j
                halves.append(small[8 + d // 4 : 9 + d // 4, c : c + FB])
            ub[0:1, 128 * t : 128 * t + 128] = jnp.concatenate(halves, axis=1)
        dub[...] = jnp.zeros_like(dub)

    n2ts[:, rows] = n2t[...]
    dys[rows, :] = dy[...]
    for c in range(4):
        cols = slice(256 * c, 256 * c + 256)
        pre = dot(n2[...], wu[:, cols], 1, 0) + ub[0:1, cols]
        dh = dot(dy[...], wd[cols, :], 1, 1)
        sq = pre * pre
        t = jnp.tanh(C0 * pre * (1.0 + C1 * sq))
        half = 0.5 + 0.5 * t
        hid = (pre * half).astype(bf16)
        slope = half + (0.5 * C0) * pre * (1.0 - t * t) * (1.0 + (3.0 * C1) * sq)
        dpre = dh * slope
        dub[0:8, cols] += fold(dpre)
        hid_o[:, cols] = hid
        ht[cols, rows] = hid.T
        dp[rows, cols] = dpre.astype(bf16)
    dn = dot(dp[rows, :], wu[...], 1, 1)
    acc_o[...] = dn if first else acc[...] + dn

    @pl.when(step == NB - 1)
    def _():
        gu[...] = dot(n2ts[...], dp[...], 1, 0).astype(bf16)
        gd[...] = dot(ht[...], dys[...], 1, 0).astype(bf16)
        scattered_rows(gu, (keep, send), offs, 0, 8, RB, 0)
        scattered_rows(gd, (keep, send), offs, 8 * RB, 6, FB, 0)


def feed_forward(j, offs, n2, n2t, dy, pieces, small, acc):
    rows = pl.BlockSpec((B, D), lambda r: (r, 0))
    extra = [] if acc is None else [rows]
    args = [] if acc is None else [acc]
    packed = pl.BlockSpec((8, FR, 128), lambda r: (0, 0, 0))
    return pl.pallas_call(
        functools.partial(ff_kernel, j=j, first=acc is None),
        grid=(NB,),
        out_shape=[
            sds((T, FC), bf16),
            sds((T, D), f32),
            sds((8, FR, 128), bf16),
            sds((8, FR, 128), bf16),
            sds((FC, D), bf16),
            sds((8, FC), f32),
        ],
        in_specs=[SM, rows, pl.BlockSpec((D, B), lambda r: (0, r)), rows]
        + [pl.BlockSpec(p.shape, lambda r: (0, 0, 0), pipeline_mode=pl.Buffered(1)) for p in pieces]
        + [pl.BlockSpec((SR, D), lambda r: (0, 0))]
        + extra,
        out_specs=[
            pl.BlockSpec((B, FC), lambda r: (r, 0)),
            rows,
            packed,
            packed,
            pl.BlockSpec((FC, D), lambda r: (0, 0)),
            pl.BlockSpec((8, FC), lambda r: (0, 0)),
        ],
        scratch_shapes=[
            pltpu.VMEM((D, FC), bf16),
            pltpu.VMEM((8, FC), f32),
            pltpu.VMEM((D, T), bf16),
            pltpu.VMEM((T, D), bf16),
            pltpu.VMEM((FC, T), bf16),
            pltpu.VMEM((T, FC), bf16),
            pltpu.VMEM((D, FC), bf16),
            pltpu.VMEM((FC, D), bf16),
        ],
        compiler_params=params(),
        cost_estimate=cost(9.7e9, 16 << 20, 1e6),
        name="feed_forward",
    )(offs, n2, n2t, dy, *pieces, small, *args)


def norm_back(v, up, gain):
    c = v - jnp.mean(v, -1, keepdims=True)
    r = lax.rsqrt(jnp.mean(c * c, -1, keepdims=True) + 1e-06)
    hat = c * r
    g = up * gain
    back = r * (g - jnp.mean(g, -1, keepdims=True) - hat * jnp.mean(g * hat, -1, keepdims=True))
    return back, up * hat


def mid_kernel(offs, dn2, x1, dy, t0, t1, t2, p0, p1, p2, p3, small,
               dx1_o, dmix_o, keep, send, sums, w, low, go):
    step = pl.program_id(0)
    rows = pl.ds(pl.multiple_of(step * B, B), B)

    @pl.when(step == 0)
    def _():
        gathered_rows(w, (p0, p1, p2, p3), offs, 0, 6, RB, 0)
        sums[...] = jnp.zeros_like(sums)

    d = dy[...].astype(f32)
    up = dn2[...]
    back, hats = norm_back(x1[...], up, small[5:6, :])
    dx1 = d + back
    dx1_o[...] = dx1
    lowered = dx1.astype(bf16)
    low[rows, :] = lowered
    sums[0:8, :] += fold(dx1)
    sums[8:16, :] += fold(hats)
    sums[16:24, :] += fold(up)
    sums[24:32, :] += fold(d)
    dmix_o[...] = dot(lowered, w[...], 1, 1).astype(bf16)

    @pl.when(step == NB - 1)
    def _():
        for g, t in enumerate((t0, t1, t2)):
            go[256 * g : 256 * g + 256, :] = dot(t[...], low[...], 1, 0).astype(bf16)
        scattered_rows(go, (keep, send), offs, 0, 6, RB, 0)


def middle(offs, dn2, x1, dy, mixts, pieces, small):
    rows = pl.BlockSpec((B, D), lambda r: (r, 0))
    packed = pl.BlockSpec((8, QR, 128), lambda r: (0, 0, 0))
    return pl.pallas_call(
        mid_kernel,
        grid=(NB,),
        out_shape=[
            sds((T, D), f32),
            sds((T, D), bf16),
            sds((8, QR, 128), bf16),
            sds((8, QR, 128), bf16),
            sds((32, D), f32),
        ],
        in_specs=[SM, rows, rows, rows]
        + [pl.BlockSpec((256, T), lambda r: (0, 0))] * 3
        + [pl.BlockSpec(p.shape, lambda r: (0, 0, 0)) for p in pieces]
        + [pl.BlockSpec((SR, D), lambda r: (0, 0))],
        out_specs=[rows, rows, packed, packed, pl.BlockSpec((32, D), lambda r: (0, 0))],
        scratch_shapes=[
            pltpu.VMEM((D, D), bf16),
            pltpu.VMEM((T, D), bf16),
            pltpu.VMEM((D, D), bf16),
        ],
        compiler_params=params(),
        cost_estimate=cost(2.4e9, 18 << 20),
        name="middle",
    )(offs, dn2, x1, dy, *mixts, *pieces, small)


def attn_bwd_kernel(
    blk, offs, q, k, v, do, mix, lse, n1t, segc, segr,
    dqkv_o, keep, send, sums, kn, vn, qt, dt, kt, qm, dm, dqt, gw,
):
    left, right = segment_tail(segc, segr, None)
    sub = lax.broadcasted_iota(jnp.int32, (16, T), 0)
    qs = q[...] * jnp.asarray(0.125, bf16)
    qtt = qs.T
    dtt = do[...].T
    kt[...] = k[...].T
    prod = (do[...].astype(f32) * mix[...].astype(f32)).T
    zero = jnp.zeros((64, T), bf16)
    pad = jnp.zeros((112, T), bf16)
    lane = lax.broadcasted_iota(jnp.int32, (T, 128), 1)
    nothing = jnp.zeros((T, 128), bf16)
    for p in range(2):
        at = slice(128 * p, 128 * p + 128)
        kn[p, :, :128] = k[:, at]
        kn[p, :, 128:] = left
        vn[p, :, :128] = v[:, at]
        vn[p, :, 128:] = left
        for e in range(2):
            h = 2 * p + e
            mine = (lane >= 64 * e) & (lane < 64 * e + 64)
            qm[p, e] = jnp.where(mine, qs[:, at], nothing)
            dm[p, e] = jnp.where(mine, do[:, at], nothing)
            for dst, src in ((qt, qtt), (dt, dtt)):
                dst[h, 64 * e : 64 * e + 64, :] = src[64 * h : 64 * h + 64]
                dst[h, 64 - 64 * e : 128 - 64 * e, :] = zero
                dst[h, 144:, :] = pad
            a, b, c = three(-lse[h : h + 1, :])
            tail = jnp.where(sub == 4, a, jnp.where(sub == 5, b, jnp.where(sub == 6, c, right)))
            qt[h, 128:144, :] = tail.astype(bf16)
            a, b, c = three(-rowsum(prod[64 * h : 64 * h + 64, :]))
            tail = jnp.where(sub == 4, a, jnp.where(sub == 5, b, jnp.where(sub == 6, c, 0.0)))
            dt[h, 128:144, :] = tail.astype(bf16)
    dqt[...] = jnp.zeros_like(dqt)
    for j in range(NB):
        lo = blk[0, j]
        hi = blk[1, j]
        keys = slice(j * B, (j + 1) * B)

        def step(i, carry):
            dks, dvs = carry
            cols = pl.ds(pl.multiple_of(i * B, B), B)
            new_dk, new_dv = [], []
            for p in range(2):
                dk, dv = dks[p], dvs[p]
                for e in range(2):
                    h = 2 * p + e
                    pr = jnp.exp(dot(kn[p, keys, :], qt[h, :, cols], 1, 0))
                    ds = (pr * dot(vn[p, keys, :], dt[h, :, cols], 1, 0)).astype(bf16)
                    dv += dot(pr.astype(bf16), dm[p, e, cols, :], 1, 0)
                    dk += dot(ds, qm[p, e, cols, :], 1, 0)
                    dqt[64 * h : 64 * h + 64, cols] += dot(kt[64 * h : 64 * h + 64, keys], ds, 1, 0)
                new_dk.append(dk)
                new_dv.append(dv)
            return tuple(new_dk), tuple(new_dv)

        zeros = tuple(jnp.zeros((B, 128), f32) for _ in range(2))
        dks, dvs = lax.fori_loop(lo, hi, step, (zeros, zeros))
        for p in range(2):
            dqkv_o[keys, 256 + 128 * p : 384 + 128 * p] = dks[p].astype(bf16)
            dqkv_o[keys, 512 + 128 * p : 640 + 128 * p] = dvs[p].astype(bf16)
    dqkv_o[:, :256] = (dqt[...] * 0.125).astype(bf16).T
    sums[:, :256] = fold(dqkv_o[:, :256].astype(f32))
    sums[:, 256:] = fold(dqkv_o[:, 512:].astype(f32))
    gw[...] = dot(n1t[...], dqkv_o[...], 1, 0).astype(bf16)
    scattered_rows(gw, (keep, send), offs, 0, 6, RB, 0)


def attn_bwd(g, blk, offs, q, k, v, dmix, mix, lse, n1t, segc, segr):
    whole = lambda a: pl.BlockSpec(a.shape, lambda r: (0,) * a.ndim)
    outs = [
        sds((T, D), bf16),
        sds((8, QR, 128), bf16),
        sds((8, QR, 128), bf16),
        sds((8, 512), f32),
    ]
    return pl.pallas_call(
        attn_bwd_kernel,
        grid=(1,),
        out_shape=outs,
        in_specs=[SM, SM, whole(q), whole(k), whole(v), pl.BlockSpec((T, 256), lambda r: (0, g))]
        + [whole(a) for a in (mix, lse, n1t, segc, segr)],
        out_specs=[whole(a) for a in outs],
        scratch_shapes=[
            pltpu.VMEM((2, T, 256), bf16),
            pltpu.VMEM((2, T, 256), bf16),
            pltpu.VMEM((4, 256, T), bf16),
            pltpu.VMEM((4, 256, T), bf16),
            pltpu.VMEM((256, T), bf16),
            pltpu.VMEM((2, 2, T, 128), bf16),
            pltpu.VMEM((2, 2, T, 128), bf16),
            pltpu.VMEM((256, T), f32),
            pltpu.VMEM((D, D), bf16),
        ],
        compiler_params=params(),
        cost_estimate=cost(16e9, 10 << 20, 4e6),
        name="attn_bwd",
    )(blk, offs, q, k, v, dmix, mix, lse, n1t, segc, segr)


def last_kernel(offs, d0, d1, d2, w0, w1, w2, x, dx1, small, mids, s0, s1, s2, u0, u1, u2,
                gt_o, keep, send, sums, sg):
    step = pl.program_id(0)

    @pl.when(step == 0)
    def _():
        sums[...] = jnp.zeros_like(sums)

    dn = dot(d0[...], w0[...], 1, 1) + dot(d1[...], w1[...], 1, 1) + dot(d2[...], w2[...], 1, 1)
    back, hats = norm_back(x[...].astype(f32), dn, small[0:1, :])
    gt_o[...] = (dx1[...] + back).astype(bf16)
    sums[0:8, :] += fold(hats)
    sums[8:16, :] += fold(dn)

    @pl.when(step == NB - 1)
    def _():
        total = lambda v: jnp.sum(v, axis=0, keepdims=True)
        sg[...] = jnp.zeros_like(sg)
        sg[0:1, :] = total(sums[0:8, :])
        sg[1:2, :] = total(sums[8:16, :])
        for g, s in enumerate((s0, s1, s2)):
            sg[2:3, 256 * g : 256 * g + 256] = total(s[:, :256])
            sg[3:4, 256 * g : 256 * g + 256] = total(s[:, 256:])
        for n in range(4):
            sg[4 + n : 5 + n, :] = total(mids[8 * n : 8 * n + 8, :])
        ups = [total(u[...]) for u in (u0, u1, u2)]
        for n in range(4):
            parts = []
            for d in range(4 * n, 4 * n + 4):
                for j in range(3):
                    parts.append(ups[j][:, FB * d : FB * d + FB])
            sg[8 + n : 9 + n, :] = jnp.concatenate(parts, axis=1)
        low = sg[...].astype(bf16)
        row = lax.broadcasted_iota(jnp.int32, (D, 128), 0)
        col = lax.broadcasted_iota(jnp.int32, (D, 128), 1)
        for s in range(OWN):
            hot = jnp.where((row == col + offs[s] * RB) & (col < RB), 1.0, 0.0).astype(bf16)
            (keep, send)[s // 8][s % 8, :, :] = dot(low, hot, 1, 0).astype(bf16)


def last_norm(offs, dqkvs, ws, x, dx1, small, mids, ssums, usums):
    rows = pl.BlockSpec((B, D), lambda r: (r, 0))
    whole = lambda a: pl.BlockSpec(a.shape, lambda r: (0,) * a.ndim)
    packed = pl.BlockSpec((8, SR, 128), lambda r: (0, 0, 0))
    return pl.pallas_call(
        last_kernel,
        grid=(NB,),
        out_shape=[sds((T, D), bf16), sds((8, SR, 128), bf16), sds((8, SR, 128), bf16)],
        in_specs=[SM] + [rows] * 3 + [whole(w) for w in ws] + [rows, rows]
        + [whole(a) for a in (small, mids, *ssums, *usums)],
        out_specs=[rows, packed, packed],
        scratch_shapes=[pltpu.VMEM((16, D), f32), pltpu.VMEM((SR, D), f32)],
        compiler_params=params(),
        cost_estimate=cost(3.6e9, 16 << 20),
        name="last_norm",
    )(offs, *dqkvs, *ws, x, dx1, small, mids, *ssums, *usums)


def out_kernel(h0, h1, h2, w0, w1, w2, x1, small, o):
    a = x1[...] + small[7:8, :]
    a += dot(h0[...], w0[...], 1, 0) + dot(h1[...], w1[...], 1, 0) + dot(h2[...], w2[...], 1, 0)
    o[...] = a.astype(bf16)


def layer_out(hids, wds, x1, small):
    rows = pl.BlockSpec((B, D), lambda r: (r, 0))
    return pl.pallas_call(
        out_kernel,
        grid=(NB,),
        out_shape=sds((T, D), bf16),
        in_specs=[pl.BlockSpec((B, FC), lambda r: (r, 0))] * 3
        + [pl.BlockSpec((FC, D), lambda r: (0, 0))] * 3
        + [rows, pl.BlockSpec((SR, D), lambda r: (0, 0))],
        out_specs=rows,
        compiler_params=params(),
        cost_estimate=cost(4.8e9, 16 << 20),
        name="layer_out",
    )(*hids, *wds, x1, small)


def adamw(weight, grad, mom_one, mom_two, rate):
    next_one = BETA1 * mom_one + (1.0 - BETA1) * grad
    next_two = BETA2 * mom_two + (1.0 - BETA2) * grad * grad
    fixed_one = next_one / (1.0 - BETA1**STEP)
    fixed_two = next_two / (1.0 - BETA2**STEP)
    updated = weight - rate * (fixed_one / (jnp.sqrt(fixed_two) + ADAM_EPS) + DECAY * weight)
    return (updated, next_one, next_two)


def adam_qkv_kernel(*refs):
    gs, (w, a, b), outs = refs[:6], refs[6:9], refs[9:12]
    for g in range(3):
        for part in range(3):
            for t in range(2):
                c = D * part + 256 * g + 128 * t
                r = (2 * part + t) * RB
                cols = slice(c, c + 128)
                grad = gs[2 * g][r : r + RB, :].astype(f32) + gs[2 * g + 1][r : r + RB, :].astype(f32)
                for o, val in zip(outs, adamw(w[:, cols], grad, a[:, cols], b[:, cols], RATES[0])):
                    o[:, cols] = val


def adam_out_kernel(g0, g1, w, a, b, *outs):
    for t in range(6):
        cols = slice(128 * t, 128 * t + 128)
        r = t * RB
        grad = g0[r : r + RB, :].astype(f32) + g1[r : r + RB, :].astype(f32)
        for o, val in zip(outs, adamw(w[:, cols], grad, a[:, cols], b[:, cols], RATES[1])):
            o[:, cols] = val


def adam_ff_kernel(*refs):
    gs = refs[:6]
    wu, au, bu, wd, ad, bd = refs[6:12]
    outs_up, outs_down = refs[12:15], refs[15:18]
    both = lambda j, r, n: gs[2 * j][r : r + n, :].astype(f32) + gs[2 * j + 1][r : r + n, :].astype(f32)
    for t in range(8):
        parts = [both(j, t * RB, RB) for j in range(3)]
        grad = jnp.concatenate([p[:, :64] for p in parts] + [p[:, 64:] for p in parts], axis=1)
        cols = slice(384 * t, 384 * t + 384)
        for o, val in zip(outs_up, adamw(wu[:, cols], grad, au[:, cols], bu[:, cols], RATES[2])):
            o[:, cols] = val
    for j in range(3):
        for t in range(6):
            grad = both(j, 8 * RB + t * FB, FB)
            at = (slice(FB * j, FB * j + FB), slice(128 * t, 128 * t + 128))
            for o, val in zip(outs_down, adamw(wd[at], grad, ad[at], bd[at], RATES[3])):
                o[at] = val


def adam_small_kernel(g0, g1, w, a, b, *outs):
    grad = g0[:12, :RB].astype(f32) + g1[:12, :RB].astype(f32)
    for o, val in zip(outs, adamw(w[...], grad, a[...], b[...], RATES[4])):
        o[...] = val


def adam_call(kernel, grads, states, name):
    shapes = [sds(s.shape, f32) for s in states]
    return pl.pallas_call(
        kernel,
        out_shape=shapes,
        in_specs=[VM] * (len(grads) + len(states)),
        out_specs=[VM] * len(shapes),
        compiler_params=params(),
        cost_estimate=cost(1e6, sum(8 * s.size for s in states)),
        name=name,
    )(*grads, *states)


def shifted(f):
    pairs = []
    for z in range(4):
        for x in range(2):
            for c in range(2):
                tz, tx, tc = f(z, x, c)
                pairs.append(((z * 2 + x) * 2 + c, (tz * 2 + tx) * 2 + tc))
    return pairs


TO_CORE = shifted(lambda z, x, c: (z, x, 1 - c))
TO_X = shifted(lambda z, x, c: (z, 1 - x, c))
TO_Z = [shifted(lambda z, x, c, s=s: ((z + s) % 4, x, c)) for s in range(4)]
FROM_Z = [shifted(lambda z, x, c, s=s: ((z - s) % 4, x, c)) for s in range(4)]
TO_Y = [(0, 1), (1, 0)]


def gather_blocks(own):
    parts = [own] + [lax.ppermute(own, "dp", TO_Z[s]) for s in (1, 2, 3)]
    line = jnp.stack(parts)
    side = lax.ppermute(line, "dp", TO_X)
    return line, side, lax.ppermute(line, "dp", TO_CORE), lax.ppermute(side, "dp", TO_CORE)


def add_first_kernel(keep, got, a, b):
    a[...] = (keep[:4].astype(f32) + got[:4].astype(f32)).astype(bf16)
    b[...] = (keep[4:].astype(f32) + got[4:].astype(f32)).astype(bf16)


def add_second_kernel(keep, got, *outs):
    for s in range(4):
        outs[s][...] = (keep[s].astype(f32) + got[s].astype(f32)).astype(bf16)


def add_third_kernel(a, b, c, d, o):
    o[...] = (a[...].astype(f32) + b[...].astype(f32) + c[...].astype(f32) + d[...].astype(f32)).astype(bf16)


def add_call(kernel, args, outs, name):
    out = pl.pallas_call(
        kernel,
        out_shape=outs,
        in_specs=[VM] * len(args),
        out_specs=[VM] * len(outs),
        compiler_params=params(),
        cost_estimate=cost(1e6, sum(2 * a.size for a in args)),
        name=name,
    )(*args)
    return out


def scatter_blocks(keep, send):
    rows = keep.shape[1]
    got = lax.ppermute(send, "dp", TO_CORE)
    mine, other = add_call(add_first_kernel, (keep, got), [sds((4, rows, 128), bf16)] * 2, "add_core")
    got = lax.ppermute(other, "dp", TO_X)
    parts = add_call(add_second_kernel, (mine, got), [sds((rows, 128), bf16)] * 4, "add_x")
    got = [lax.ppermute(parts[s], "dp", FROM_Z[s]) for s in (1, 2, 3)]
    (own,) = add_call(add_third_kernel, (parts[0], *got), [sds((rows, 128), bf16)], "add_z")
    return own, lax.ppermute(own, "rep", TO_Y)


def gather_any(small, wq, wo, wu, wd):
    full = lambda w, axis: lax.all_gather(w.astype(bf16), "dp", axis=axis, tiled=True)
    small = full(small, 1)
    blocks = small.reshape(small.shape[0], OWN, RB).transpose(1, 0, 2)
    blocks = jnp.pad(blocks, ((0, 0), (0, SR - small.shape[0]), (0, 128 - RB)))
    q = full(wq, 0).reshape(OWN, RB, 3, 3, 2, 128).transpose(3, 0, 2, 4, 1, 5).reshape(3, OWN, QR, 128)
    o = full(wo, 0).reshape(OWN, RB, 6, 128).transpose(0, 2, 1, 3).reshape(OWN, QR, 128)
    u = full(wu, 0).reshape(OWN, RB, 8, 2, 3, FB).transpose(4, 0, 2, 1, 3, 5).reshape(3, OWN, 8 * RB, 128)
    d = full(wd, 0).reshape(OWN, 3, FB, 6, 128).transpose(1, 0, 3, 2, 4).reshape(3, OWN, 6 * FB, 128)
    f = jnp.concatenate([u, d], 2)
    first = jnp.concatenate([q[0], blocks], 1)
    cut = lambda a: tuple(a[4 * n : 4 * n + 4] for n in range(4))
    return cut(first), cut(q[1]), cut(q[2]), cut(o), cut(f[0]), cut(f[1]), cut(f[2])


def scatter_any(packs):
    q0, q1, q2, o, f0, f1, f2, s = [jnp.concatenate(p, 0) for p in packs]
    q = jnp.stack([q0, q1, q2]).reshape(3, OWN, 3, 2, RB, 128).transpose(1, 4, 2, 0, 3, 5)
    f = jnp.stack([f0, f1, f2])
    u = f[:, :, : 8 * RB].reshape(3, OWN, 8, RB, 2, FB).transpose(1, 3, 2, 4, 0, 5)
    d = f[:, :, 8 * RB :].reshape(3, OWN, 6, FB, 128).transpose(1, 0, 3, 2, 4)
    o = o.reshape(OWN, 6, RB, 128).transpose(0, 2, 1, 3)
    s = s[:, :12, :RB].transpose(1, 0, 2).reshape(12, D)
    flat = ((q.reshape(D, 3 * D), 0), (o.reshape(D, D), 0), (u.reshape(D, FF), 0), (d.reshape(FF, D), 0), (s, 1))
    out = []
    for g, axis in flat:
        g = lax.psum_scatter(g, "dp", scatter_dimension=axis, tiled=True)
        out.append(lax.psum(g, "rep").astype(f32))
    return out


def shards(tokens, segment_ids, cotangent, *state, wide):
    masters, firsts, seconds = state[:5], state[5:10], state[10:15]
    w_qkv, w_out, w_up, w_down, small_params = masters
    x = tokens[0]
    dy = cotangent[0]
    seg = segment_ids[0]
    segc = seg.reshape(T, 1)
    segr = seg.reshape(1, T)
    begins, ends = seg[::B], seg[B - 1 :: B]
    low = jnp.sum(ends[None, :] < begins[:, None], 1)
    high = jnp.sum(begins[None, :] <= ends[:, None], 1)
    blk = jnp.stack([low, high]).astype(jnp.int32)

    if wide:
        me = lax.axis_index("dp")
        s = jnp.arange(OWN, dtype=jnp.int32)
        z = (me // 4 - s % 4) % 4
        xx = (me // 2 % 2) ^ (s // 4 % 2)
        cc = (me % 2) ^ (s // 8)
        offs = ((z * 2 + xx) * 2 + cc).astype(jnp.int32)
        owns = pack(small_params, w_qkv, w_out, w_up, w_down)
        pieces = [gather_blocks(own) for own in owns]
    else:
        offs = jnp.arange(OWN, dtype=jnp.int32)
        pieces = gather_any(small_params, w_qkv, w_out, w_up, w_down)

    n1, n1t, small = norm_first(offs, x, pieces[0], QR)
    fwd = [attn_fwd(g, blk, offs, n1, pieces[g], small, segc, segr) for g in range(3)]
    x1, n2, n2t = post_attn(offs, x, [f[3] for f in fwd], pieces[3], small)
    acc = None
    ffs = []
    for j in range(3):
        hid, acc, keep, send, wd, dub = feed_forward(j, offs, n2, n2t, dy, pieces[4 + j], small, acc)
        ffs.append((hid, keep, send, wd, dub))
    dx1, dmix, keep_o, send_o, mids = middle(offs, acc, x1, dy, [f[4] for f in fwd], pieces[3], small)
    bwd = []
    for g in range(3):
        q, k, v, mix, _, lse, _ = fwd[g]
        bwd.append(attn_bwd(g, blk, offs, q, k, v, dmix, mix, lse, n1t, segc, segr))
    grad_tokens, keep_s, send_s = last_norm(
        offs, [b[0] for b in bwd], [f[6] for f in fwd], x, dx1, small, mids,
        [b[3] for b in bwd], [f[4] for f in ffs],
    )
    result = layer_out([f[0] for f in ffs], [f[3] for f in ffs], x1, small)
    packs = [(b[1], b[2]) for b in bwd] + [(keep_o, send_o)] + [(f[1], f[2]) for f in ffs] + [(keep_s, send_s)]
    states = [(masters[n], firsts[n], seconds[n]) for n in range(5)]
    if wide:
        done = [scatter_blocks(*p) for p in packs]
        flat = lambda items: [a for pair in items for a in pair]
        new = [None] * 5
        new[0] = adam_call(adam_qkv_kernel, flat(done[:3]), states[0], "adam_qkv")
        new[1] = adam_call(adam_out_kernel, done[3], states[1], "adam_out")
        both = adam_call(adam_ff_kernel, flat(done[4:7]), states[2] + states[3], "adam_ff")
        new[2], new[3] = both[:3], both[3:]
        new[4] = adam_call(adam_small_kernel, done[7], states[4], "adam_small")
    else:
        owned = scatter_any(packs)
        new = [adamw(states[n][0], owned[n], states[n][1], states[n][2], RATES[n]) for n in range(5)]
    return (
        result[None],
        grad_tokens[None],
        *[n[0] for n in new],
        *[n[1] for n in new],
        *[n[2] for n in new],
    )


def solution(mesh):
    rows = P("dp", None)
    small = P(None, "dp")
    state = (rows, rows, rows, rows, small)
    seqs = P(("dp", "rep"), None, None)
    return jax.shard_map(
        functools.partial(shards, wide=mesh.shape["dp"] == 16 and mesh.shape["rep"] == 2),
        mesh=mesh,
        in_specs=(seqs, P(("dp", "rep"), None), seqs) + state * 3,
        out_specs=(seqs, seqs) + state * 3,
        check_vma=False,
    )
```

time: 904 us -> 529 us (0.59)
  matrix products: 292 us -> 0 us
  waiting for transfers between devices: 393 us -> 115 us
  Pallas kernels: 0 us -> 248 us
  starting transfers between devices: 0.41 us -> 143 us
  other arithmetic: 108 us -> 3.55 us
  local copies, waits for them, and re-layouts: 53.9 us -> 12.1 us
  blocking collectives: 28.2 us -> 0 us
  between operations: 15.1 us -> 1.71 us
    dot_general x96 -> x0, matrix products: 292 us -> none  [the longest x40 104 us: outer_rows(): lax.dot_general(left, right, (((1,), (1,)), ((), ())), preferred_element_...]
    reduce_scatter x4 -> x0, waiting for transfers between devices: 266 us -> none  [the longest x1 114 us: shards(): lax.psum_scatter(grad_up, 'dp', scatter_dimension=0, tiled=True)]
    pallas_call x0 -> x43, Pallas kernels: none -> 248 us  [the longest x3 60.2 us: feed_forward(): pl.pallas_call(functools.partial(ff_kernel, j=j, first=acc is None), grid...]
    ppermute x0 -> x90, starting transfers between devices: none -> 143 us  [the longest x24 49.7 us: scatter_blocks(): got = [lax.ppermute(parts[s], 'dp', FROM_Z[s]) for s in (1, 2, 3)]]
    ppermute x0 -> x90, waiting for transfers between devices: none -> 115 us  [the longest x8 36.4 us: scatter_blocks(): got = lax.ppermute(other, 'dp', TO_X)]
    reduce_sum x45 -> x1, other arithmetic: 55.3 us -> 0.21 us  [shards(): low = jnp.sum(ends[None, :] < begins[:, None], 1)]
    all_gather x4 -> x0, waiting for transfers between devices: 50.8 us -> none  [the longest x1 32.7 us: shards(): lax.all_gather(w_down.astype(bf16), 'dp', axis=0, tiled=True)]
    convert_element_type x23 -> x0, other arithmetic: 44 us -> none  [the longest x12 27.2 us: head_backward(): grad_scores = pull_soft(grad_probs)[0].astype(bf16)]
  transfers between devices with their start and end apart: 10 -> 90, of which waited for: 7 -> 27; matrix products, arithmetic and copies ran while one was open for 45% -> 1% of each run, Pallas kernels for 0% -> 46%
where the time goes in v1:
time: 529 us; the launch traced here: 523 us
  Pallas kernels  248 us (47%)
  starting transfers between devices  143 us (27%)
  waiting for transfers between devices  115 us (22%)
  local copies, waits for them, and re-layouts  12.1 us (2%)
    pallas_call x3, Pallas kernels, feed_forward(): pl.pallas_call(functools.partial(ff_kernel, j=j, first=acc is None), grid...  60.2 us
    ppermute x24, starting transfers between devices, scatter_blocks(): got = [lax.ppermute(parts[s], 'dp', FROM_Z[s]) for s in (1, 2, 3)]  49.7 us
    pallas_call x3, Pallas kernels, attn_bwd(): pl.pallas_call(attn_bwd_kernel, grid=(1,), out_shape=outs, in_specs=[SM,...  49.6 us
    pallas_call x24, Pallas kernels, add_call(): pl.pallas_call(kernel, out_shape=outs, in_specs=[VM] * len(args), out_spe...  49 us
    ppermute x21, starting transfers between devices, gather_blocks(): parts = [own] + [lax.ppermute(own, 'dp', TO_Z[s]) for s in (1, 2, 3)]  45.3 us
    ppermute x8, waiting for transfers between devices, scatter_blocks(): got = lax.ppermute(other, 'dp', TO_X)  36.4 us
    pallas_call x3, Pallas kernels, attn_fwd(): pl.pallas_call(functools.partial(attn_fwd_kernel, g=g), out_shape=[sds((T...  33 us
    ppermute x21, waiting for transfers between devices, gather_blocks(): parts = [own] + [lax.ppermute(own, 'dp', TO_Z[s]) for s in (1, 2, 3)]  30.5 us
  transfers between devices with their start and end apart: 90, of which 27 were waited for; matrix products, arithmetic and copies ran while one was open for 1% of the time, Pallas kernels for 46%

profile of v1, /device:TPU:0, one launch (start us, length us, event | category | flops | bytes accessed | tf_op | source)
XLA Modules:
  0.0 523.1 jit_solution(6641681842255766208)
XLA Ops:
  4.4 5.1 collective-permute-start.8
  30.7 13.0 %collective-permute-start.24 = (bf16[768,128]{1,0:T(8,128)(2,1)}, bf16[768,128]{1,0:T(8,128)(2,1)S(1)}, u32[]{:S(2)}, u32[]{:S(2)}) collective-permute-start(bf16[768,128]{1,0:T(8,128)(2,1)} %get-tuple-element.163), channel_id=1, source_target_pairs={{0,8},{2,10},{4,12},{6,14},{8,16},{10,18},{12,20},{14,22},{16,24},... | collective-permute-start | bytes 589832 | tf_op jit(solution)/shard_map/ppermute | solution.py:732
  51.1 4.6 collective-permute-start.32
  62.7 10.2 %collective-permute-done.31 = bf16[768,128]{1,0:T(8,128)(2,1)S(1)} collective-permute-done((bf16[768,128]{1,0:T(8,128)(2,1)S(1)}, bf16[768,128]{1,0:T(8,128)(2,1)S(1)}, u32[]{:S(2)}, u32[]{:S(2)}) %collective-permute-start.31) | collective-permute-done | bytes 196640 | tf_op jit(solution)/shard_map/ppermute | solution.py:732
  75.1 13.4 %collective-permute-done.37 = bf16[768,128]{1,0:T(8,128)(2,1)S(1)} collective-permute-done((bf16[768,128]{1,0:T(8,128)(2,1)S(1)}, bf16[768,128]{1,0:T(8,128)(2,1)S(1)}, u32[]{:S(2)}, u32[]{:S(2)}) %collective-permute-start.37) | collective-permute-done | bytes 196640 | tf_op jit(solution)/shard_map/ppermute | solution.py:732
  91.7 5.1 norm_first.1
  96.8 10.8 %attn_fwd.3 = (bf16[1024,256]{1,0:T(8,128)(2,1)}, bf16[1024,256]{1,0:T(8,128)(2,1)}, bf16[1024,256]{1,0:T(8,128)(2,1)}, bf16[1024,256]{1,0:T(8,128)(2,1)}, bf16[...) custom-call(s32[2,4]{1,0:T(2,128)} %pad_add_fusion.blk, s32[16]{0:T(128)} %fusion.1.offs.refs_0_, ...), custom_call_target="tpu_custom_call" | custom-call | flops 8999999488 | bytes 8388608 | tf_op jit(solution)/shard_map/attn_fwd/pallas_call | solution.py:243
  107.8 4.0 collective-permute-start.27
  112.6 11.1 %attn_fwd.5 = (bf16[1024,256]{1,0:T(8,128)(2,1)}, bf16[1024,256]{1,0:T(8,128)(2,1)}, bf16[1024,256]{1,0:T(8,128)(2,1)}, bf16[1024,256]{1,0:T(8,128)(2,1)}, bf16[...) custom-call(s32[2,4]{1,0:T(2,128)} %pad_add_fusion.blk, s32[16]{0:T(128)} %fusion.1.offs.refs_0_, ...), custom_call_target="tpu_custom_call" | custom-call | flops 8999999488 | bytes 8388608 | tf_op jit(solution)/shard_map/attn_fwd/pallas_call | solution.py:243
  126.5 3.6 collective-permute-done.27.refs_5_
  130.2 11.1 %attn_fwd.4 = (bf16[1024,256]{1,0:T(8,128)(2,1)}, bf16[1024,256]{1,0:T(8,128)(2,1)}, bf16[1024,256]{1,0:T(8,128)(2,1)}, bf16[1024,256]{1,0:T(8,128)(2,1)}, bf16[...) custom-call(s32[2,4]{1,0:T(2,128)} %pad_add_fusion.blk, s32[16]{0:T(128)} %fusion.1.offs.refs_0_, ...), custom_call_target="tpu_custom_call" | custom-call | flops 8999999488 | bytes 8388608 | tf_op jit(solution)/shard_map/attn_fwd/pallas_call | solution.py:243
  142.1 6.5 %post_attn.1 = (f32[1024,768]{1,0:T(8,128)}, bf16[1024,768]{1,0:T(8,128)(2,1)}, bf16[768,1024]{1,0:T(8,128)(2,1)}) custom-call(s32[16]{0:T(128)} %fusion.1.offs.refs_0_, bf16[1024,768]{1,0:T(8,128)(2,1)} %bitcast.37, bf16[1024,256]{1,0:T(8,128)(2,1)} %get-tuple-element.155.m0.mix, bf16[1024,256]{1,0:T(8,128)(2,1)} %get-tuple-element.157.m1.mix, ...), custom_call_target="tpu_custom_call" | custom-call | flops 1200000000 | bytes 10485760 | tf_op jit(solution)/shard_map/post_attn/pallas_call | solution.py:280
  148.9 14.5 %collective-permute-done.33.refs_5_ = bf16[4,768,128]{2,1,0:T(8,128)(2,1)S(1)} collective-permute-done((bf16[4,768,128]{2,1,0:T(8,128)(2,1)S(1)}, bf16[4,768,128]{2,1,0:T(8,128)(2,1)S(1)}, u32[]{:S(2)}, u32[]{:S(2)}) %collective-permute-start.33) | collective-permute-done | bytes 786464 | tf_op jit(solution)/shard_map/ppermute | solution.py:734
  164.3 16.8 %feed_forward.3 = (bf16[1024,1024]{1,0:T(8,128)(2,1)}, f32[1024,768]{1,0:T(8,128)}, bf16[8,768,128]{2,1,0:T(8,128)(2,1)}, bf16[8,768,128]{2,1,0:T(8,128)(2,1)}, ...) custom-call(s32[16]{0:T(128)} %fusion.1.offs.refs_0_, bf16[1024,768]{1,0:T(8,128)(2,1)} %get-tuple-element.161.refs_1_, ...), custom_call_target="tpu_custom_call" | custom-call | flops 9699999744 | bytes 16777216 | tf_op jit(solution)/shard_map/feed_forward/pallas_call | solution.py:355
  182.8 17.2 %feed_forward.4 = (bf16[1024,1024]{1,0:T(8,128)(2,1)}, f32[1024,768]{1,0:T(8,128)}, bf16[8,768,128]{2,1,0:T(8,128)(2,1)}, bf16[8,768,128]{2,1,0:T(8,128)(2,1)}, ...) custom-call(s32[16]{0:T(128)} %fusion.1.offs.refs_0_, bf16[1024,768]{1,0:T(8,128)(2,1)} %get-tuple-element.161.refs_1_, ...), custom_call_target="tpu_custom_call" | custom-call | flops 9699999744 | bytes 16777216 | tf_op jit(solution)/shard_map/feed_forward/pallas_call | solution.py:355
  200.2 26.2 %feed_forward.5 = (bf16[1024,1024]{1,0:T(8,128)(2,1)}, f32[1024,768]{1,0:T(8,128)}, bf16[8,768,128]{2,1,0:T(8,128)(2,1)}, bf16[8,768,128]{2,1,0:T(8,128)(2,1)}, ...) custom-call(s32[16]{0:T(128)} %fusion.1.offs.refs_0_, bf16[1024,768]{1,0:T(8,128)(2,1)} %get-tuple-element.161.refs_1_, ...), custom_call_target="tpu_custom_call" | custom-call | flops 9699999744 | bytes 16777216 | tf_op jit(solution)/shard_map/feed_forward/pallas_call | solution.py:355
  226.4 10.9 %middle.1 = (f32[1024,768]{1,0:T(8,128)}, bf16[1024,768]{1,0:T(8,128)(2,1)}, bf16[8,288,128]{2,1,0:T(8,128)(2,1)}, bf16[8,288,128]{2,1,0:T(8,128)(2,1)}, f32[32,768]{1,0:T(8,128)}) custom-call(s32[16]{0:T(128)} %fusion.1.offs.refs_0_, f32[1024,768]{1,0:T(8,128)} %get-tuple-element.178.dn2, f32[1024,768]{1,0:T(8,128)} %get-tuple-element.174.x1, ...), custom_call_target="tpu_custom_call" | custom-call | flops 2400000000 | bytes 18874368 | tf_op jit(solution)/shard_map/middle/pallas_call | solution.py:436
  237.9 16.8 %attn_bwd.5 = (bf16[1024,768]{1,0:T(8,128)(2,1)}, bf16[8,288,128]{2,1,0:T(8,128)(2,1)}, bf16[8,288,128]{2,1,0:T(8,128)(2,1)}, f32[8,512]{1,0:T(8,128)}) custom-call(s32[2,4]{1,0:T(2,128)} %pad_add_fusion.blk, s32[16]{0:T(128)} %fusion.1.offs.refs_0_, bf16[1024,256]{1,0:T(8,128)(2,1)} %get-tuple-element.191.q, bf16[1024,256]{1,0:T(8,128)(2,1)} %get-tuple-element.192.k, ...), custom_call_target="tpu_custom_call" | custom-call | flops 16000000000 | bytes 10485760 | tf_op jit(solution)/shard_map/attn_bwd/pallas_call | solution.py:541
  254.7 16.3 %attn_bwd.4 = (bf16[1024,768]{1,0:T(8,128)(2,1)}, bf16[8,288,128]{2,1,0:T(8,128)(2,1)}, bf16[8,288,128]{2,1,0:T(8,128)(2,1)}, f32[8,512]{1,0:T(8,128)}) custom-call(s32[2,4]{1,0:T(2,128)} %pad_add_fusion.blk, s32[16]{0:T(128)} %fusion.1.offs.refs_0_, bf16[1024,256]{1,0:T(8,128)(2,1)} %get-tuple-element.186.q, bf16[1024,256]{1,0:T(8,128)(2,1)} %get-tuple-element.187.k, ...), custom_call_target="tpu_custom_call" | custom-call | flops 16000000000 | bytes 10485760 | tf_op jit(solution)/shard_map/attn_bwd/pallas_call | solution.py:541
  271.0 16.5 %attn_bwd.3 = (bf16[1024,768]{1,0:T(8,128)(2,1)}, bf16[8,288,128]{2,1,0:T(8,128)(2,1)}, bf16[8,288,128]{2,1,0:T(8,128)(2,1)}, f32[8,512]{1,0:T(8,128)}) custom-call(s32[2,4]{1,0:T(2,128)} %pad_add_fusion.blk, s32[16]{0:T(128)} %fusion.1.offs.refs_0_, bf16[1024,256]{1,0:T(8,128)(2,1)} %get-tuple-element.175.q, bf16[1024,256]{1,0:T(8,128)(2,1)} %get-tuple-element.176.k, ...), custom_call_target="tpu_custom_call" | custom-call | flops 16000000000 | bytes 10485760 | tf_op jit(solution)/shard_map/attn_bwd/pallas_call | solution.py:541
  287.5 10.5 %last_norm.1 = (bf16[1024,768]{1,0:T(8,128)(2,1)}, bf16[8,16,128]{2,1,0:T(8,128)(2,1)}, bf16[8,16,128]{2,1,0:T(8,128)(2,1)}) custom-call(s32[16]{0:T(128)} %fusion.1.offs.refs_0_, bf16[1024,768]{1,0:T(8,128)(2,1)} %get-tuple-element.185.d0, bf16[1024,768]{1,0:T(8,128)(2,1)} %get-tuple-element.190.d1, bf16[1024,768]{1,0:T(8,128)(2,1)} %get-tuple-element.195.d2, ...), custom_call_target="tpu_custom_call" | custom-call | flops 3600000000 | bytes 16777216 | tf_op jit(solution)/shard_map/last_norm/pallas_call | solution.py:609
  301.6 15.5 %collective-permute-start.85 = (bf16[4,16,128]{2,1,0:T(8,128)(2,1)}, bf16[4,16,128]{2,1,0:T(8,128)(2,1)S(1)}, u32[]{:S(2)}, u32[]{:S(2)}) collective-permute-start(bf16[4,16,128]{2,1,0:T(8,128)(2,1)} %get-tuple-element.271), channel_id=1, source_target_pairs={{0,4},{2,6},{4,0},{6,2},{8,12},{10,14},{12,8},{14,10},{16,20},{18,... | collective-permute-start | bytes 49160 | tf_op jit(solution)/shard_map/ppermute | solution.py:769
  331.7 4.1 collective-permute-done.88.d
  366.6 29.9 %collective-permute-done.49.got = bf16[4,288,128]{2,1,0:T(8,128)(2,1)S(1)} collective-permute-done((bf16[4,288,128]{2,1,0:T(8,128)(2,1)}, bf16[4,288,128]{2,1,0:T(8,128)(2,1)S(1)}, u32[]{:S(2)}, u32[]{:S(2)}) %collective-permute-start.49) | collective-permute-done | bytes 294944 | tf_op jit(solution)/shard_map/ppermute | solution.py:769
  398.2 4.6 collective-permute-done.43.got
  441.2 3.8 collective-permute-start.74
  445.0 6.1 %collective-permute-start.75 = (bf16[768,128]{1,0:T(8,128)(2,1)}, bf16[768,128]{1,0:T(8,128)(2,1)S(1)}, u32[]{:S(2)}, u32[]{:S(2)}) collective-permute-start(bf16[768,128]{1,0:T(8,128)(2,1)} %get-tuple-element.256), channel_id=1, source_target_pairs={{0,16},{2,18},{4,20},{6,22},{8,24},{10,26},{12,28},{14,30},{16,0},... | collective-permute-start | bytes 589832 | tf_op jit(solution)/shard_map/ppermute | solution.py:771
  451.1 3.8 collective-permute-start.76
  457.2 5.6 %collective-permute-done.69.c = bf16[768,128]{1,0:T(8,128)(2,1)S(1)} collective-permute-done((bf16[768,128]{1,0:T(8,128)(2,1)}, bf16[768,128]{1,0:T(8,128)(2,1)S(1)}, u32[]{:S(2)}, u32[]{:S(2)}) %collective-permute-start.69) | collective-permute-done | bytes 196640 | tf_op jit(solution)/shard_map/ppermute | solution.py:771
  465.8 10.3 %collective-permute-start.82 = (bf16[768,128]{1,0:T(8,128)(2,1)}, bf16[768,128]{1,0:T(8,128)(2,1)S(1)}, u32[]{:S(2)}, u32[]{:S(2)}) collective-permute-start(bf16[768,128]{1,0:T(8,128)(2,1)} %get-tuple-element.265), channel_id=1, source_target_pairs={{0,8},{2,10},{4,12},{6,14},{8,16},{10,18},{12,20},{14,22},{16,24},... | collective-permute-start | bytes 589832 | tf_op jit(solution)/shard_map/ppermute | solution.py:771
  499.2 10.1 %layer_out.1 = bf16[1024,768]{1,0:T(8,128)(2,1)} custom-call(bf16[1024,1024]{1,0:T(8,128)(2,1)} %get-tuple-element.164.h0, bf16[1024,1024]{1,0:T(8,128)(2,1)} %get-tuple-element.167.h1, bf16[1024,1024]{1,0:T(8,128)(2,1)} %get-tuple-element.170.h2, bf16[1024,768]{1,0:T(8,128)(2,1)} %get-tuple-element.171.w0, bf16[1024,768]{1,0:T(8,128)(2,1)} %get-tuple-element.172.w1, ...), custom_call_target="tpu_custom_call" | custom-call | flops 4800000000 | bytes 16777216 | tf_op jit(solution)/shard_map/layer_out/pallas_call | solution.py:631
  518.2 4.7 adam_ff.1
  (373 shorter events, 178.7 us)
Async XLA Ops:
  29.8 25.9 %collective-permute-start.26 = (bf16[768,128]{1,0:T(8,128)(2,1)}, bf16[768,128]{1,0:T(8,128)(2,1)S(1)}, u32[]{:S(2)}, u32[]{:S(2)}) collective-permute-start(bf16[768,128]{1,0:T(8,128)(2,1)} %get-tuple-element.163), channel_id=1, source_target_pairs={{0,24},{2,26},{4,28},{6,30},{8,0},{10,2},{12,4},{14,6},{16,8},{18,... | collective-permute-start | bytes 589832 | tf_op jit(solution)/shard_map/ppermute | solution.py:732
  30.7 25.0 %collective-permute-start.25 = (bf16[768,128]{1,0:T(8,128)(2,1)}, bf16[768,128]{1,0:T(8,128)(2,1)S(1)}, u32[]{:S(2)}, u32[]{:S(2)}) collective-permute-start(bf16[768,128]{1,0:T(8,128)(2,1)} %get-tuple-element.163), channel_id=1, source_target_pairs={{0,16},{2,18},{4,20},{6,22},{8,24},{10,26},{12,28},{14,30},{16,0},... | collective-permute-start | bytes 589832 | tf_op jit(solution)/shard_map/ppermute | solution.py:732
  30.7 26.2 %collective-permute-start.24 = (bf16[768,128]{1,0:T(8,128)(2,1)}, bf16[768,128]{1,0:T(8,128)(2,1)S(1)}, u32[]{:S(2)}, u32[]{:S(2)}) collective-permute-start(bf16[768,128]{1,0:T(8,128)(2,1)} %get-tuple-element.163), channel_id=1, source_target_pairs={{0,8},{2,10},{4,12},{6,14},{8,16},{10,18},{12,20},{14,22},{16,24},... | collective-permute-start | bytes 589832 | tf_op jit(solution)/shard_map/ppermute | solution.py:732
  45.5 28.8 %collective-permute-start.3 = (bf16[4,304,128]{2,1,0:T(8,128)(2,1)S(1)}, bf16[4,304,128]{2,1,0:T(8,128)(2,1)S(1)}, u32[]{:S(2)}, u32[]{:S(2)}) collective-permute-start(bf16[4,304,128]{2,1,0:T(8,128)(2,1)S(1)} %pad_maximum_fusion.3.p0), channel_id=1, source_target_pairs={{0,4},{2,6},{4,0},{6,2},{8,12},{10,14},{12,8},{14,10},{16,20},{18,... | collective-permute-start | bytes 933896 | tf_op jit(solution)/shard_map/ppermute | solution.py:734
  61.1 27.4 %collective-permute-start.37 = (bf16[768,128]{1,0:T(8,128)(2,1)S(1)}, bf16[768,128]{1,0:T(8,128)(2,1)S(1)}, u32[]{:S(2)}, u32[]{:S(2)}) collective-permute-start(bf16[768,128]{1,0:T(8,128)(2,1)S(1)} %copy-done.33), channel_id=1, source_target_pairs={{0,16},{2,18},{4,20},{6,22},{8,24},{10,26},{12,28},{14,30},{16,0},... | collective-permute-start | bytes 589832 | tf_op jit(solution)/shard_map/ppermute | solution.py:732
  88.5 35.2 %collective-permute-start.22 = (bf16[4,288,128]{2,1,0:T(8,128)(2,1)S(1)}, bf16[4,288,128]{2,1,0:T(8,128)(2,1)S(1)}, u32[]{:S(2)}, u32[]{:S(2)}) collective-permute-start(bf16[4,288,128]{2,1,0:T(8,128)(2,1)S(1)} %pad_maximum_fusion.6.p0), channel_id=1, source_target_pairs={{0,2},{2,0},{4,6},{6,4},{8,10},{10,8},{12,14},{14,12},{16,18},{18,... | collective-permute-start | bytes 884744 | tf_op jit(solution)/shard_map/ppermute | solution.py:735
  88.5 35.3 %collective-permute-start.21 = (bf16[4,288,128]{2,1,0:T(8,128)(2,1)S(1)}, bf16[4,288,128]{2,1,0:T(8,128)(2,1)S(1)}, u32[]{:S(2)}, u32[]{:S(2)}) collective-permute-start(bf16[4,288,128]{2,1,0:T(8,128)(2,1)S(1)} %pad_maximum_fusion.6.p0), channel_id=1, source_target_pairs={{0,4},{2,6},{4,0},{6,2},{8,12},{10,14},{12,8},{14,10},{16,20},{18,... | collective-permute-start | bytes 884744 | tf_op jit(solution)/shard_map/ppermute | solution.py:734
  90.9 20.9 %collective-permute-start.17 = (bf16[4,288,128]{2,1,0:T(8,128)(2,1)S(1)}, bf16[4,288,128]{2,1,0:T(8,128)(2,1)S(1)}, u32[]{:S(2)}, u32[]{:S(2)}) collective-permute-start(bf16[4,288,128]{2,1,0:T(8,128)(2,1)S(1)} %collective-permute-done.15.p1), channel_id=1, source_target_pairs={{0,2},{2,0},{4,6},{6,4},{8,10},{10,8},{12,14},{14,12},{16,18},{18,... | collective-permute-start | bytes 884744 | tf_op jit(solution)/shard_map/ppermute | solution.py:735
  107.8 22.4 %collective-permute-start.27 = (bf16[4,768,128]{2,1,0:T(8,128)(2,1)S(1)}, bf16[4,768,128]{2,1,0:T(8,128)(2,1)S(1)}, u32[]{:S(2)}, u32[]{:S(2)}) collective-permute-start(bf16[4,768,128]{2,1,0:T(8,128)(2,1)S(1)} %pad_maximum_fusion.refs_4_), channel_id=1, source_target_pairs={{0,4},{2,6},{4,0},{6,2},{8,12},{10,14},{12,8},{14,10},{16,20},{18,... | collective-permute-start | bytes 2359304 | tf_op jit(solution)/shard_map/ppermute | solution.py:734
  123.7 39.7 %collective-permute-start.28 = (bf16[4,768,128]{2,1,0:T(8,128)(2,1)S(1)}, bf16[4,768,128]{2,1,0:T(8,128)(2,1)S(1)}, u32[]{:S(2)}, u32[]{:S(2)}) collective-permute-start(bf16[4,768,128]{2,1,0:T(8,128)(2,1)S(1)} %pad_maximum_fusion.refs_4_), channel_id=1, source_target_pairs={{0,2},{2,0},{4,6},{6,4},{8,10},{10,8},{12,14},{14,12},{16,18},{18,... | collective-permute-start | bytes 2359304 | tf_op jit(solution)/shard_map/ppermute | solution.py:735
  123.8 24.8 %collective-permute-start.39 = (bf16[4,768,128]{2,1,0:T(8,128)(2,1)S(1)}, bf16[4,768,128]{2,1,0:T(8,128)(2,1)S(1)}, u32[]{:S(2)}, u32[]{:S(2)}) collective-permute-start(bf16[4,768,128]{2,1,0:T(8,128)(2,1)S(1)} %pad_maximum_fusion.2.refs_4_), channel_id=1, source_target_pairs={{0,4},{2,6},{4,0},{6,2},{8,12},{10,14},{12,8},{14,10},{16,20},{18,... | collective-permute-start | bytes 2359304 | tf_op jit(solution)/shard_map/ppermute | solution.py:734
  126.4 36.9 %collective-permute-start.33 = (bf16[4,768,128]{2,1,0:T(8,128)(2,1)S(1)}, bf16[4,768,128]{2,1,0:T(8,128)(2,1)S(1)}, u32[]{:S(2)}, u32[]{:S(2)}) collective-permute-start(bf16[4,768,128]{2,1,0:T(8,128)(2,1)S(1)} %pad_maximum_fusion.1.refs_4_), channel_id=1, source_target_pairs={{0,4},{2,6},{4,0},{6,2},{8,12},{10,14},{12,8},{14,10},{16,20},{18,... | collective-permute-start | bytes 2359304 | tf_op jit(solution)/shard_map/ppermute | solution.py:734
  130.2 33.7 %collective-permute-start.29 = (bf16[4,768,128]{2,1,0:T(8,128)(2,1)S(1)}, bf16[4,768,128]{2,1,0:T(8,128)(2,1)}, u32[]{:S(2)}, u32[]{:S(2)}) collective-permute-start(bf16[4,768,128]{2,1,0:T(8,128)(2,1)S(1)} %collective-permute-done.27.refs_5_), channel_id=1, source_target_pairs={{0,2},{2,0},{4,6},{6,4},{8,10},{10,8},{12,14},{14,12},{16,18},{18,... | collective-permute-start | bytes 2359304 | tf_op jit(solution)/shard_map/ppermute | solution.py:735
  141.4 58.8 %collective-permute-start.40 = (bf16[4,768,128]{2,1,0:T(8,128)(2,1)S(1)}, bf16[4,768,128]{2,1,0:T(8,128)(2,1)}, u32[]{:S(2)}, u32[]{:S(2)}) collective-permute-start(bf16[4,768,128]{2,1,0:T(8,128)(2,1)S(1)} %pad_maximum_fusion.2.refs_4_), channel_id=1, source_target_pairs={{0,2},{2,0},{4,6},{6,4},{8,10},{10,8},{12,14},{14,12},{16,18},{18,... | collective-permute-start | bytes 2359304 | tf_op jit(solution)/shard_map/ppermute | solution.py:735
  148.6 33.1 %collective-permute-start.34 = (bf16[4,768,128]{2,1,0:T(8,128)(2,1)S(1)}, bf16[4,768,128]{2,1,0:T(8,128)(2,1)S(1)}, u32[]{:S(2)}, u32[]{:S(2)}) collective-permute-start(bf16[4,768,128]{2,1,0:T(8,128)(2,1)S(1)} %pad_maximum_fusion.1.refs_4_), channel_id=1, source_target_pairs={{0,2},{2,0},{4,6},{6,4},{8,10},{10,8},{12,14},{14,12},{16,18},{18,... | collective-permute-start | bytes 2359304 | tf_op jit(solution)/shard_map/ppermute | solution.py:735
  163.4 36.8 %collective-permute-start.41 = (bf16[4,768,128]{2,1,0:T(8,128)(2,1)S(1)}, bf16[4,768,128]{2,1,0:T(8,128)(2,1)}, u32[]{:S(2)}, u32[]{:S(2)}) collective-permute-start(bf16[4,768,128]{2,1,0:T(8,128)(2,1)S(1)} %collective-permute-done.39.refs_5_), channel_id=1, source_target_pairs={{0,2},{2,0},{4,6},{6,4},{8,10},{10,8},{12,14},{14,12},{16,18},{18,... | collective-permute-start | bytes 2359304 | tf_op jit(solution)/shard_map/ppermute | solution.py:735
  181.1 163.2 %collective-permute-start.66 = (bf16[8,768,128]{2,1,0:T(8,128)(2,1)}, bf16[8,768,128]{2,1,0:T(8,128)(2,1)S(1)}, u32[]{:S(2)}, u32[]{:S(2)}) collective-permute-start(bf16[8,768,128]{2,1,0:T(8,128)(2,1)} %get-tuple-element.243), channel_id=1, source_target_pairs={{0,2},{2,0},{4,6},{6,4},{8,10},{10,8},{12,14},{14,12},{16,18},{18,... | collective-permute-start | bytes 4718600 | tf_op jit(solution)/shard_map/ppermute | solution.py:767
  200.1 148.6 %collective-permute-start.72 = (bf16[8,768,128]{2,1,0:T(8,128)(2,1)}, bf16[8,768,128]{2,1,0:T(8,128)(2,1)S(1)}, u32[]{:S(2)}, u32[]{:S(2)}) collective-permute-start(bf16[8,768,128]{2,1,0:T(8,128)(2,1)} %get-tuple-element.251), channel_id=1, source_target_pairs={{0,2},{2,0},{4,6},{6,4},{8,10},{10,8},{12,14},{14,12},{16,18},{18,... | collective-permute-start | bytes 4718600 | tf_op jit(solution)/shard_map/ppermute | solution.py:767
  237.3 98.5 %collective-permute-start.60 = (bf16[8,288,128]{2,1,0:T(8,128)(2,1)}, bf16[8,288,128]{2,1,0:T(8,128)(2,1)S(1)}, u32[]{:S(2)}, u32[]{:S(2)}) collective-permute-start(bf16[8,288,128]{2,1,0:T(8,128)(2,1)} %get-tuple-element.234), channel_id=1, source_target_pairs={{0,2},{2,0},{4,6},{6,4},{8,10},{10,8},{12,14},{14,12},{16,18},{18,... | collective-permute-start | bytes 1769480 | tf_op jit(solution)/shard_map/ppermute | solution.py:767
  237.8 121.6 %collective-permute-start.78 = (bf16[8,768,128]{2,1,0:T(8,128)(2,1)}, bf16[8,768,128]{2,1,0:T(8,128)(2,1)S(1)}, u32[]{:S(2)}, u32[]{:S(2)}) collective-permute-start(bf16[8,768,128]{2,1,0:T(8,128)(2,1)} %get-tuple-element.259), channel_id=1, source_target_pairs={{0,2},{2,0},{4,6},{6,4},{8,10},{10,8},{12,14},{14,12},{16,18},{18,... | collective-permute-start | bytes 4718600 | tf_op jit(solution)/shard_map/ppermute | solution.py:767
  348.7 82.9 %collective-permute-start.67 = (bf16[4,768,128]{2,1,0:T(8,128)(2,1)}, bf16[4,768,128]{2,1,0:T(8,128)(2,1)S(1)}, u32[]{:S(2)}, u32[]{:S(2)}) collective-permute-start(bf16[4,768,128]{2,1,0:T(8,128)(2,1)} %get-tuple-element.245), channel_id=1, source_target_pairs={{0,4},{2,6},{4,0},{6,2},{8,12},{10,14},{12,8},{14,10},{16,20},{18,... | collective-permute-start | bytes 2359304 | tf_op jit(solution)/shard_map/ppermute | solution.py:769
  353.1 84.8 %collective-permute-start.73 = (bf16[4,768,128]{2,1,0:T(8,128)(2,1)}, bf16[4,768,128]{2,1,0:T(8,128)(2,1)S(1)}, u32[]{:S(2)}, u32[]{:S(2)}) collective-permute-start(bf16[4,768,128]{2,1,0:T(8,128)(2,1)} %get-tuple-element.253), channel_id=1, source_target_pairs={{0,4},{2,6},{4,0},{6,2},{8,12},{10,14},{12,8},{14,10},{16,20},{18,... | collective-permute-start | bytes 2359304 | tf_op jit(solution)/shard_map/ppermute | solution.py:769
  356.2 40.3 %collective-permute-start.49 = (bf16[4,288,128]{2,1,0:T(8,128)(2,1)}, bf16[4,288,128]{2,1,0:T(8,128)(2,1)S(1)}, u32[]{:S(2)}, u32[]{:S(2)}) collective-permute-start(bf16[4,288,128]{2,1,0:T(8,128)(2,1)} %get-tuple-element.219), channel_id=1, source_target_pairs={{0,4},{2,6},{4,0},{6,2},{8,12},{10,14},{12,8},{14,10},{16,20},{18,... | collective-permute-start | bytes 884744 | tf_op jit(solution)/shard_map/ppermute | solution.py:769
  359.4 43.4 %collective-permute-start.43 = (bf16[4,288,128]{2,1,0:T(8,128)(2,1)}, bf16[4,288,128]{2,1,0:T(8,128)(2,1)S(1)}, u32[]{:S(2)}, u32[]{:S(2)}) collective-permute-start(bf16[4,288,128]{2,1,0:T(8,128)(2,1)} %get-tuple-element.211), channel_id=1, source_target_pairs={{0,4},{2,6},{4,0},{6,2},{8,12},{10,14},{12,8},{14,10},{16,20},{18,... | collective-permute-start | bytes 884744 | tf_op jit(solution)/shard_map/ppermute | solution.py:769
  363.8 81.1 %collective-permute-start.79 = (bf16[4,768,128]{2,1,0:T(8,128)(2,1)}, bf16[4,768,128]{2,1,0:T(8,128)(2,1)S(1)}, u32[]{:S(2)}, u32[]{:S(2)}) collective-permute-start(bf16[4,768,128]{2,1,0:T(8,128)(2,1)} %get-tuple-element.261), channel_id=1, source_target_pairs={{0,4},{2,6},{4,0},{6,2},{8,12},{10,14},{12,8},{14,10},{16,20},{18,... | collective-permute-start | bytes 2359304 | tf_op jit(solution)/shard_map/ppermute | solution.py:769
  437.8 25.0 %collective-permute-start.69 = (bf16[768,128]{1,0:T(8,128)(2,1)}, bf16[768,128]{1,0:T(8,128)(2,1)S(1)}, u32[]{:S(2)}, u32[]{:S(2)}) collective-permute-start(bf16[768,128]{1,0:T(8,128)(2,1)} %get-tuple-element.248), channel_id=1, source_target_pairs={{0,16},{2,18},{4,20},{6,22},{8,24},{10,26},{12,28},{14,30},{16,0},... | collective-permute-start | bytes 589832 | tf_op jit(solution)/shard_map/ppermute | solution.py:771
  441.1 21.7 %collective-permute-start.70 = (bf16[768,128]{1,0:T(8,128)(2,1)S(1)}, bf16[768,128]{1,0:T(8,128)(2,1)S(1)}, u32[]{:S(2)}, u32[]{:S(2)}) collective-permute-start(bf16[768,128]{1,0:T(8,128)(2,1)S(1)} %copy-done.83), channel_id=1, source_target_pairs={{0,8},{2,10},{4,12},{6,14},{8,16},{10,18},{12,20},{14,22},{16,24},... | collective-permute-start | bytes 589832 | tf_op jit(solution)/shard_map/ppermute | solution.py:771
  441.2 24.6 %collective-permute-start.74 = (bf16[768,128]{1,0:T(8,128)(2,1)}, bf16[768,128]{1,0:T(8,128)(2,1)S(1)}, u32[]{:S(2)}, u32[]{:S(2)}) collective-permute-start(bf16[768,128]{1,0:T(8,128)(2,1)} %get-tuple-element.255), channel_id=1, source_target_pairs={{0,24},{2,26},{4,28},{6,30},{8,0},{10,2},{12,4},{14,6},{16,8},{18,... | collective-permute-start | bytes 589832 | tf_op jit(solution)/shard_map/ppermute | solution.py:771
  445.0 34.7 %collective-permute-start.75 = (bf16[768,128]{1,0:T(8,128)(2,1)}, bf16[768,128]{1,0:T(8,128)(2,1)S(1)}, u32[]{:S(2)}, u32[]{:S(2)}) collective-permute-start(bf16[768,128]{1,0:T(8,128)(2,1)} %get-tuple-element.256), channel_id=1, source_target_pairs={{0,16},{2,18},{4,20},{6,22},{8,24},{10,26},{12,28},{14,30},{16,0},... | collective-permute-start | bytes 589832 | tf_op jit(solution)/shard_map/ppermute | solution.py:771
  451.1 30.4 %collective-permute-start.76 = (bf16[768,128]{1,0:T(8,128)(2,1)}, bf16[768,128]{1,0:T(8,128)(2,1)S(1)}, u32[]{:S(2)}, u32[]{:S(2)}) collective-permute-start(bf16[768,128]{1,0:T(8,128)(2,1)} %get-tuple-element.257), channel_id=1, source_target_pairs={{0,8},{2,10},{4,12},{6,14},{8,16},{10,18},{12,20},{14,22},{16,24},... | collective-permute-start | bytes 589832 | tf_op jit(solution)/shard_map/ppermute | solution.py:771
  462.9 29.5 %collective-permute-start.81 = (bf16[768,128]{1,0:T(8,128)(2,1)}, bf16[768,128]{1,0:T(8,128)(2,1)S(1)}, u32[]{:S(2)}, u32[]{:S(2)}) collective-permute-start(bf16[768,128]{1,0:T(8,128)(2,1)} %get-tuple-element.264), channel_id=1, source_target_pairs={{0,16},{2,18},{4,20},{6,22},{8,24},{10,26},{12,28},{14,30},{16,0},... | collective-permute-start | bytes 589832 | tf_op jit(solution)/shard_map/ppermute | solution.py:771
  465.8 26.8 %collective-permute-start.82 = (bf16[768,128]{1,0:T(8,128)(2,1)}, bf16[768,128]{1,0:T(8,128)(2,1)S(1)}, u32[]{:S(2)}, u32[]{:S(2)}) collective-permute-start(bf16[768,128]{1,0:T(8,128)(2,1)} %get-tuple-element.265), channel_id=1, source_target_pairs={{0,8},{2,10},{4,12},{6,14},{8,16},{10,18},{12,20},{14,22},{16,24},... | collective-permute-start | bytes 589832 | tf_op jit(solution)/shard_map/ppermute | solution.py:771
  (142 other events, 2372.3 us)
